TPU v7x, 32 devices: a whole 2x2x4 slice. The times are simulated.
32 devices in a mesh: owner: 2 (over x), ctx: 16 (over z, y, core).
Axes of the slice: x: 2, y: 2, z: 4, core: 2. Of those that a mesh axis runs over, the one named last changes fastest.
Arguments:
- span_cache: bfloat16 [256, 128, 1024], P(('owner', 'ctx')), may hold values from -8 to 8
- retrieval: int32 [2, 128], P(None, 'ctx'), may hold values from 0 to 255, as said below
- counts: int32 [2], replicated, may hold values from 32 to 128, as said below
- recompute_pos: int32 [2, 128], P('owner'), may hold values from 0 to 1023, as said below
- hidden: bfloat16 [2, 128, 8192], P('owner', None, 'ctx'), may hold values from -6 to 6
- kv_weight: bfloat16 [8192, 1024], P('ctx'), may hold values from -0.0625 to 0.0625
- queries: bfloat16 [2, 128, 4096], P('owner', 'ctx'), may hold values from -8 to 8
- block_mask: int32 [2, 128, 128], P('owner', None, 'ctx'), may hold values from 0 to 1, as said below
Outputs:
- context_kv: bfloat16 [2, 16384, 1024], P('owner', 'ctx')
- attended: bfloat16 [2, 128, 4096], P('owner', 'ctx')
Inputs may be any that keep to these rules, and one draw needn't show every extreme that they name: `retrieval`: the span for block b of a request is stored on index b // 8 of ctx of some owner group o: its number is (o * 16 + b // 8) * 8 + s. Among the 8 blocks of one request on one index of ctx at most 4 name spans of one owner group, and in every draw some reach 4. `counts`: some request uses all 128 blocks in every draw. `recompute_pos`: the 8 positions of one request on one index of ctx are distinct. `block_mask`: every query block may see itself and those of the first 4 blocks not after it; no block sees a later one.
All inputs are finite; a program needn't handle non-finite values.
Results may differ from a plain program's by a relative error of at most 0.023.
Values may be sent and summed in bfloat16 or wider, within the bound.
A program may use at most 128 MiB of HBM per device.

v0:
```python
import jax
import jax.numpy as jnp
from jax import lax
from jax.sharding import PartitionSpec as P

QH = 32
KVH = 4
HD = 128
BLK = 128
NBD = 8
RCP = 8
SLOTS = 8
CAP = 4
CTX_DEV = 1024


def passed_along(shard, axis, by):
    peers = lax.axis_size(axis)
    return lax.ppermute(shard, axis, [(i, (i + by) % peers) for i in range(peers)])


def absorb(
    query_rows,
    query_pos,
    numerator,
    running,
    totals_now,
    key_rows,
    value_rows,
    key_pos,
    key_in_use,
    mask_cols,
):
    row_count = query_rows.shape[0]
    per_group = QH // KVH
    allowed = jnp.take(mask_cols, query_pos // BLK, axis=0)
    visible = jnp.repeat(allowed, BLK, axis=1) > 0
    visible = visible & key_in_use[None, :] & (key_pos[None, :] <= query_pos[:, None])
    grouped = query_rows.reshape(row_count, KVH, per_group, HD)
    scores = jnp.einsum(
        "rkgd,tkd->kgrt", grouped, key_rows, preferred_element_type=jnp.float32
    ) * HD ** (-0.5)
    scores = jnp.where(visible[None, None], scores, -1e30)
    running = running.reshape(KVH, per_group, row_count)
    newest = jnp.maximum(running, jnp.max(scores, axis=3))
    weights = jnp.where(visible[None, None], jnp.exp(scores - newest[..., None]), 0.0)
    factor = jnp.exp(running - newest)
    totals_now = totals_now.reshape(KVH, per_group, row_count) * factor + jnp.sum(weights, axis=3)
    weighted = jnp.einsum(
        "kgrt,tkd->rkgd",
        weights.astype(jnp.bfloat16),
        value_rows,
        preferred_element_type=jnp.float32,
    )
    numerator = (
        numerator.reshape(row_count, KVH, per_group, HD)
        * jnp.transpose(factor, (2, 0, 1))[..., None]
        + weighted
    )
    return (
        numerator.reshape(row_count, QH * HD),
        newest.reshape(QH, row_count),
        totals_now.reshape(QH, row_count),
    )


def on_device(span_cache, retrieval, counts, recompute_pos, hidden, kv_weight, queries, block_mask):
    owner_count = lax.axis_size("owner")
    cycle_size = lax.axis_size("ctx")
    my_owner = lax.axis_index("owner")
    my_ctx = lax.axis_index("ctx")
    feature_count = span_cache.shape[2]
    positions = jnp.arange(NBD, dtype=jnp.int32)
    block_ids = my_ctx * NBD + positions
    in_use = block_ids[None, :] < counts[:, None]
    holder = retrieval // (cycle_size * SLOTS)
    outbound = in_use & (holder == my_owner)
    slot_rank = jnp.cumsum(outbound.astype(jnp.int32), axis=1) - 1
    picked = outbound[:, None, :] & (
        slot_rank[:, None, :] == jnp.arange(CAP, dtype=jnp.int32)[None, :, None]
    )
    chosen = jnp.sum(jnp.where(picked, (retrieval % SLOTS)[:, None, :], 0), axis=2)
    filled = jnp.any(picked, axis=2)
    outgoing = jnp.where(
        filled[:, :, None, None], jnp.take(span_cache, chosen, axis=0), jnp.zeros((), jnp.bfloat16)
    )
    arrived = lax.all_to_all(outgoing, "owner", split_axis=0, concat_axis=0, tiled=True)
    wanted = lax.dynamic_index_in_dim(retrieval, my_owner, 0, keepdims=False)
    my_count = lax.dynamic_index_in_dim(counts, my_owner, 0, keepdims=False)
    my_in_use = block_ids < my_count
    source = wanted // (cycle_size * SLOTS)
    earlier = (
        (source[:, None] == source[None, :])
        & my_in_use[None, :]
        & (positions[None, :] < positions[:, None])
    )
    ordinal = jnp.sum(earlier.astype(jnp.int32), axis=1)
    flattened = arrived.reshape(owner_count * CAP, BLK, feature_count)
    blocks = jnp.take(flattened, source * CAP + ordinal, axis=0, mode="clip")
    blocks = jnp.where(my_in_use[:, None, None], blocks, jnp.zeros((), jnp.bfloat16))
    context = blocks.reshape(CTX_DEV, feature_count)
    local_rows = hidden[0]
    recomputed = lax.psum_scatter(
        jnp.dot(local_rows, kv_weight, preferred_element_type=jnp.float32).astype(jnp.bfloat16),
        "ctx",
        scatter_dimension=0,
        tiled=True,
    )
    every_pos = recompute_pos[0]
    own_pos = lax.dynamic_slice_in_dim(every_pos, my_ctx * RCP, RCP)
    matches = jnp.arange(CTX_DEV, dtype=jnp.int32)[:, None] == own_pos[None, :]
    placed = jnp.dot(
        matches.astype(jnp.bfloat16), recomputed, preferred_element_type=jnp.float32
    ).astype(jnp.bfloat16)
    context = jnp.where(jnp.any(matches, axis=1)[:, None], placed, context)
    key_width = KVH * HD
    key_rows = context[:, :key_width].reshape(CTX_DEV, KVH, HD)
    value_rows = context[:, key_width:].reshape(CTX_DEV, KVH, HD)
    key_pos = my_ctx * CTX_DEV + jnp.arange(CTX_DEV, dtype=jnp.int32)
    key_in_use = key_pos // BLK < my_count
    mask_cols = block_mask[0]
    query_starts = jnp.arange(cycle_size * RCP, dtype=jnp.int32) // RCP * CTX_DEV + every_pos
    numerator_zero = jnp.zeros((RCP, QH * HD), jnp.float32)
    running_zero = jnp.full((QH, RCP), -1e30, jnp.float32)
    totals_zero = jnp.zeros((QH, RCP), jnp.float32)

    def visit_keys(query_rows, offset, numerator, running, totals_now):
        query_pos = lax.dynamic_slice_in_dim(query_starts, offset, query_rows.shape[0])
        return absorb(
            query_rows,
            query_pos,
            numerator,
            running,
            totals_now,
            key_rows,
            value_rows,
            key_pos,
            key_in_use,
            mask_cols,
        )

    def pass_state(carried):
        return passed_along(carried, "ctx", 1)

    def cycle_turn(turn_index, carry):
        visiting, numerator, running, totals_now = carry
        source_index = (my_ctx - turn_index) % cycle_size
        carried = visit_keys(visiting, source_index * RCP, numerator, running, totals_now)
        visiting = passed_along(visiting, "ctx", 1)
        numerator, running, totals_now = pass_state(carried)
        return (visiting, numerator, running, totals_now)

    visiting, numerator, running, totals_now = lax.fori_loop(
        0, cycle_size - 1, cycle_turn, (queries[0], numerator_zero, running_zero, totals_zero)
    )
    source_index = (my_ctx - (cycle_size - 1)) % cycle_size
    carried = visit_keys(visiting, source_index * RCP, numerator, running, totals_now)
    numerator, running, totals_now = pass_state(carried)
    result = numerator.reshape(RCP, QH, HD) / jnp.transpose(totals_now)[:, :, None]
    attended = result.reshape(RCP, QH * HD).astype(jnp.bfloat16)
    return (context[None], attended[None])


def solution(mesh):
    in_specs = (
        P(("owner", "ctx"), None, None),
        P(None, "ctx"),
        P(),
        P("owner", None),
        P("owner", None, "ctx"),
        P("ctx", None),
        P("owner", "ctx", None),
        P("owner", None, "ctx"),
    )
    out_specs = (P("owner", "ctx", None), P("owner", "ctx", None))
    return jax.shard_map(
        on_device, mesh=mesh, in_specs=in_specs, out_specs=out_specs, check_vma=False
    )
```

profile of v0, /device:TPU:0, one launch (start us, length us, event | category | flops | bytes accessed | tf_op | source)
XLA Modules:
  0.0 349.1 jit_solution(8811735858368144527)
XLA Ops:
  9.4 2.0 gather_fusion.1
  11.4 3.2 select_select_fusion.1
  14.6 4.9 %all-to-all-start = ((bf16[2,4,128,1024]{3,2,1,0:T(8,128)(2,1)}), bf16[2,4,128,1024]{3,2,1,0:T(8,128)(2,1)}, u32[]{:S(2)}, u32[]{:S(2)}) async-start(bf16[2,4,128,1024]{3,2,1,0:T(8,128)(2,1)} %select_select_fusion.1), calls=%async_computation.1 | async-start | bytes 4194304 | tf_op jit(solution)/shard_map/all_to_all | solution.py:87
  27.4 18.6 %all-to-all-done = bf16[2,4,128,1024]{3,2,1,0:T(8,128)(2,1)} async-done(((bf16[2,4,128,1024]{3,2,1,0:T(8,128)(2,1)}), bf16[2,4,128,1024]{3,2,1,0:T(8,128)(2,1)}, u32[]{:S(2)}, u32[]{:S(2)}) %all-to-all-start) | async-done | bytes 2097184 | tf_op jit(solution)/shard_map/all_to_all | solution.py:87
  46.0 3.6 %gather_fusion.2 = bf16[8,128,1024]{2,1,0:T(8,128)(2,1)} fusion(bf16[8,128,1024]{2,1,0:T(8,128)(2,1)} %bitcast.6, s32[1024]{0:T(1024)S(1)} %pad_clamp_fusion.2), kind=kCustom, calls=%fused_computation.3 | custom fusion | bytes 4194336 | tf_op jit(solution)/shard_map/jit(_take)/gather | solution.py:99
  49.6 3.9 %copy.125 = bf16[1024,1024]{0,1:T(8,128)(2,1)} copy(bf16[1024,1024]{1,0:T(8,128)(2,1)} %bitcast.162) | data formatting | bytes 4194304 | tf_op jit(solution)/shard_map/jit(_take)/gather | solution.py:99
  53.6 28.9 %reduce-scatter.2.cloned.1.call-done = bf16[8,1024]{1,0:T(8,128)(2,1)} async-done(((bf16[128,1024]{1,0:T(8,128)(2,1)}), bf16[8,1024]{1,0:T(8,128)(2,1)}) %reduce-scatter.2.cloned.1.call-update) | async-done | bytes 16400 | tf_op jit(solution)/shard_map/reduce_scatter | solution.py:103
  82.5 2.4 select_select_fusion
  84.9 1.6 fusion.51
  86.9 1.6 copy.107
  88.6 2.3 copy.108
  92.0 236.8 %while.23 = (s32[]{:T(128)}, bf16[8,4096]{1,0:T(8,128)(2,1)S(1)}, f32[8,4096]{1,0:T(8,128)S(1)}, f32[32,8]{0,1:T(8,128)}, f32[32,8]{0,1:T(8,128)}, /*index=5*/s3...) while((s32[]{:T(128)}, bf16[8,4096]{1,0:T(8,128)(2,1)S(1)}, ...), condition=%wide.region_9.11_spmd.clone.clone, body=%wide.region_6.10_spmd.clone.clone.sunk | while | flops 136687936 | bytes 11293444 | solution.py:153
  97.5 1.5 collective-permute-start.1
  104.4 4.3 %collective-permute-done.2 = f32[32,8]{0,1:T(8,128)} collective-permute-done((f32[32,8]{0,1:T(8,128)S(1)}, f32[32,8]{0,1:T(8,128)}, u32[]{:S(2)}, u32[]{:S(2)}) %collective-permute-start.2) | collective-permute-done | bytes 1056 | tf_op jit(solution)/shard_map/while/body/eval_jaxpr/ppermute | solution.py:19
  119.8 4.6 %collective-permute-done.2 = f32[32,8]{0,1:T(8,128)} collective-permute-done((f32[32,8]{0,1:T(8,128)S(1)}, f32[32,8]{0,1:T(8,128)}, u32[]{:S(2)}, u32[]{:S(2)}) %collective-permute-start.2) | collective-permute-done | bytes 1056 | tf_op jit(solution)/shard_map/while/body/eval_jaxpr/ppermute | solution.py:19
  134.2 5.8 %collective-permute-done.2 = f32[32,8]{0,1:T(8,128)} collective-permute-done((f32[32,8]{0,1:T(8,128)S(1)}, f32[32,8]{0,1:T(8,128)}, u32[]{:S(2)}, u32[]{:S(2)}) %collective-permute-start.2) | collective-permute-done | bytes 1056 | tf_op jit(solution)/shard_map/while/body/eval_jaxpr/ppermute | solution.py:19
  149.9 5.8 %collective-permute-done.2 = f32[32,8]{0,1:T(8,128)} collective-permute-done((f32[32,8]{0,1:T(8,128)S(1)}, f32[32,8]{0,1:T(8,128)}, u32[]{:S(2)}, u32[]{:S(2)}) %collective-permute-start.2) | collective-permute-done | bytes 1056 | tf_op jit(solution)/shard_map/while/body/eval_jaxpr/ppermute | solution.py:19
  165.6 5.8 %collective-permute-done.2 = f32[32,8]{0,1:T(8,128)} collective-permute-done((f32[32,8]{0,1:T(8,128)S(1)}, f32[32,8]{0,1:T(8,128)}, u32[]{:S(2)}, u32[]{:S(2)}) %collective-permute-start.2) | collective-permute-done | bytes 1056 | tf_op jit(solution)/shard_map/while/body/eval_jaxpr/ppermute | solution.py:19
  181.3 5.8 %collective-permute-done.2 = f32[32,8]{0,1:T(8,128)} collective-permute-done((f32[32,8]{0,1:T(8,128)S(1)}, f32[32,8]{0,1:T(8,128)}, u32[]{:S(2)}, u32[]{:S(2)}) %collective-permute-start.2) | collective-permute-done | bytes 1056 | tf_op jit(solution)/shard_map/while/body/eval_jaxpr/ppermute | solution.py:19
  197.0 5.8 %collective-permute-done.2 = f32[32,8]{0,1:T(8,128)} collective-permute-done((f32[32,8]{0,1:T(8,128)S(1)}, f32[32,8]{0,1:T(8,128)}, u32[]{:S(2)}, u32[]{:S(2)}) %collective-permute-start.2) | collective-permute-done | bytes 1056 | tf_op jit(solution)/shard_map/while/body/eval_jaxpr/ppermute | solution.py:19
  212.7 5.8 %collective-permute-done.2 = f32[32,8]{0,1:T(8,128)} collective-permute-done((f32[32,8]{0,1:T(8,128)S(1)}, f32[32,8]{0,1:T(8,128)}, u32[]{:S(2)}, u32[]{:S(2)}) %collective-permute-start.2) | collective-permute-done | bytes 1056 | tf_op jit(solution)/shard_map/while/body/eval_jaxpr/ppermute | solution.py:19
  228.4 5.8 %collective-permute-done.2 = f32[32,8]{0,1:T(8,128)} collective-permute-done((f32[32,8]{0,1:T(8,128)S(1)}, f32[32,8]{0,1:T(8,128)}, u32[]{:S(2)}, u32[]{:S(2)}) %collective-permute-start.2) | collective-permute-done | bytes 1056 | tf_op jit(solution)/shard_map/while/body/eval_jaxpr/ppermute | solution.py:19
  244.0 5.8 %collective-permute-done.2 = f32[32,8]{0,1:T(8,128)} collective-permute-done((f32[32,8]{0,1:T(8,128)S(1)}, f32[32,8]{0,1:T(8,128)}, u32[]{:S(2)}, u32[]{:S(2)}) %collective-permute-start.2) | collective-permute-done | bytes 1056 | tf_op jit(solution)/shard_map/while/body/eval_jaxpr/ppermute | solution.py:19
  259.7 5.8 %collective-permute-done.2 = f32[32,8]{0,1:T(8,128)} collective-permute-done((f32[32,8]{0,1:T(8,128)S(1)}, f32[32,8]{0,1:T(8,128)}, u32[]{:S(2)}, u32[]{:S(2)}) %collective-permute-start.2) | collective-permute-done | bytes 1056 | tf_op jit(solution)/shard_map/while/body/eval_jaxpr/ppermute | solution.py:19
  275.4 5.8 %collective-permute-done.2 = f32[32,8]{0,1:T(8,128)} collective-permute-done((f32[32,8]{0,1:T(8,128)S(1)}, f32[32,8]{0,1:T(8,128)}, u32[]{:S(2)}, u32[]{:S(2)}) %collective-permute-start.2) | collective-permute-done | bytes 1056 | tf_op jit(solution)/shard_map/while/body/eval_jaxpr/ppermute | solution.py:19
  291.1 5.8 %collective-permute-done.2 = f32[32,8]{0,1:T(8,128)} collective-permute-done((f32[32,8]{0,1:T(8,128)S(1)}, f32[32,8]{0,1:T(8,128)}, u32[]{:S(2)}, u32[]{:S(2)}) %collective-permute-start.2) | collective-permute-done | bytes 1056 | tf_op jit(solution)/shard_map/while/body/eval_jaxpr/ppermute | solution.py:19
  306.8 5.8 %collective-permute-done.2 = f32[32,8]{0,1:T(8,128)} collective-permute-done((f32[32,8]{0,1:T(8,128)S(1)}, f32[32,8]{0,1:T(8,128)}, u32[]{:S(2)}, u32[]{:S(2)}) %collective-permute-start.2) | collective-permute-done | bytes 1056 | tf_op jit(solution)/shard_map/while/body/eval_jaxpr/ppermute | solution.py:19
  322.5 5.8 %collective-permute-done.2 = f32[32,8]{0,1:T(8,128)} collective-permute-done((f32[32,8]{0,1:T(8,128)S(1)}, f32[32,8]{0,1:T(8,128)}, u32[]{:S(2)}, u32[]{:S(2)}) %collective-permute-start.2) | collective-permute-done | bytes 1056 | tf_op jit(solution)/shard_map/while/body/eval_jaxpr/ppermute | solution.py:19
  329.6 1.7 fusion.52
  332.7 1.6 fusion.24
  335.0 3.9 %copy.120 = bf16[1,1024,1024]{2,1,0:T(8,128)(2,1)} copy(bf16[1,1024,1024]{1,2,0:T(8,128)(2,1)} %bitcast.161) | data formatting | bytes 4194304
  339.0 2.5 collective-permute-done.5
  (553 shorter events, 164.8 us)
Async XLA Ops:
  14.6 31.4 %all-to-all-start = ((bf16[2,4,128,1024]{3,2,1,0:T(8,128)(2,1)}), bf16[2,4,128,1024]{3,2,1,0:T(8,128)(2,1)}, u32[]{:S(2)}, u32[]{:S(2)}) async-start(bf16[2,4,128,1024]{3,2,1,0:T(8,128)(2,1)} %select_select_fusion.1), calls=%async_computation.1 | async-start | bytes 4194304 | tf_op jit(solution)/shard_map/all_to_all | solution.py:87
  19.6 62.9 %reduce-scatter.2.cloned.1.call-start = ((), (), s32[]{:S(2)}) async-start(), calls=%async_computation.2 | async-start | bytes 278528 | tf_op jit(solution)/shard_map/reduce_scatter | solution.py:103
  92.0 16.6 %collective-permute-start = (bf16[8,4096]{1,0:T(8,128)(2,1)S(1)}, bf16[8,4096]{1,0:T(8,128)(2,1)S(1)}, u32[]{:S(2)}, u32[]{:S(2)}) collective-permute-start(bf16[8,4096]{1,0:T(8,128)(2,1)S(1)} %copy.183), channel_id=1, source_target_pairs={{0,1},{1,2},{2,3},{3,4},{4,5},{5,6},{6,7},{7,8},{8,9},{9,10},{10,1... | collective-permute-start | bytes 196616 | tf_op jit(solution)/shard_map/while/body/eval_jaxpr/ppermute | solution.py:19
  97.5 11.1 %collective-permute-start.1 = (f32[8,4096]{1,0:T(8,128)S(1)}, f32[8,4096]{1,0:T(8,128)S(1)}, u32[]{:S(2)}, u32[]{:S(2)}) collective-permute-start(f32[8,4096]{1,0:T(8,128)S(1)} %bitcast.168), channel_id=1, source_target_pairs={{0,1},{1,2},{2,3},{3,4},{4,5},{5,6},{6,7},{7,8},{8,9},{9,10},{10,1... | collective-permute-start | bytes 393224 | tf_op jit(solution)/shard_map/while/body/eval_jaxpr/ppermute | solution.py:19
  109.2 15.1 %collective-permute-start = (bf16[8,4096]{1,0:T(8,128)(2,1)S(1)}, bf16[8,4096]{1,0:T(8,128)(2,1)S(1)}, u32[]{:S(2)}, u32[]{:S(2)}) collective-permute-start(bf16[8,4096]{1,0:T(8,128)(2,1)S(1)} %copy.183), channel_id=1, source_target_pairs={{0,1},{1,2},{2,3},{3,4},{4,5},{5,6},{6,7},{7,8},{8,9},{9,10},{10,1... | collective-permute-start | bytes 196616 | tf_op jit(solution)/shard_map/while/body/eval_jaxpr/ppermute | solution.py:19
  114.7 9.7 %collective-permute-start.1 = (f32[8,4096]{1,0:T(8,128)S(1)}, f32[8,4096]{1,0:T(8,128)S(1)}, u32[]{:S(2)}, u32[]{:S(2)}) collective-permute-start(f32[8,4096]{1,0:T(8,128)S(1)} %bitcast.168), channel_id=1, source_target_pairs={{0,1},{1,2},{2,3},{3,4},{4,5},{5,6},{6,7},{7,8},{8,9},{9,10},{10,1... | collective-permute-start | bytes 393224 | tf_op jit(solution)/shard_map/while/body/eval_jaxpr/ppermute | solution.py:19
  124.9 15.1 %collective-permute-start = (bf16[8,4096]{1,0:T(8,128)(2,1)S(1)}, bf16[8,4096]{1,0:T(8,128)(2,1)S(1)}, u32[]{:S(2)}, u32[]{:S(2)}) collective-permute-start(bf16[8,4096]{1,0:T(8,128)(2,1)S(1)} %copy.183), channel_id=1, source_target_pairs={{0,1},{1,2},{2,3},{3,4},{4,5},{5,6},{6,7},{7,8},{8,9},{9,10},{10,1... | collective-permute-start | bytes 196616 | tf_op jit(solution)/shard_map/while/body/eval_jaxpr/ppermute | solution.py:19
  130.4 9.7 %collective-permute-start.1 = (f32[8,4096]{1,0:T(8,128)S(1)}, f32[8,4096]{1,0:T(8,128)S(1)}, u32[]{:S(2)}, u32[]{:S(2)}) collective-permute-start(f32[8,4096]{1,0:T(8,128)S(1)} %bitcast.168), channel_id=1, source_target_pairs={{0,1},{1,2},{2,3},{3,4},{4,5},{5,6},{6,7},{7,8},{8,9},{9,10},{10,1... | collective-permute-start | bytes 393224 | tf_op jit(solution)/shard_map/while/body/eval_jaxpr/ppermute | solution.py:19
  140.6 15.1 %collective-permute-start = (bf16[8,4096]{1,0:T(8,128)(2,1)S(1)}, bf16[8,4096]{1,0:T(8,128)(2,1)S(1)}, u32[]{:S(2)}, u32[]{:S(2)}) collective-permute-start(bf16[8,4096]{1,0:T(8,128)(2,1)S(1)} %copy.183), channel_id=1, source_target_pairs={{0,1},{1,2},{2,3},{3,4},{4,5},{5,6},{6,7},{7,8},{8,9},{9,10},{10,1... | collective-permute-start | bytes 196616 | tf_op jit(solution)/shard_map/while/body/eval_jaxpr/ppermute | solution.py:19
  146.1 9.7 %collective-permute-start.1 = (f32[8,4096]{1,0:T(8,128)S(1)}, f32[8,4096]{1,0:T(8,128)S(1)}, u32[]{:S(2)}, u32[]{:S(2)}) collective-permute-start(f32[8,4096]{1,0:T(8,128)S(1)} %bitcast.168), channel_id=1, source_target_pairs={{0,1},{1,2},{2,3},{3,4},{4,5},{5,6},{6,7},{7,8},{8,9},{9,10},{10,1... | collective-permute-start | bytes 393224 | tf_op jit(solution)/shard_map/while/body/eval_jaxpr/ppermute | solution.py:19
  156.3 15.1 %collective-permute-start = (bf16[8,4096]{1,0:T(8,128)(2,1)S(1)}, bf16[8,4096]{1,0:T(8,128)(2,1)S(1)}, u32[]{:S(2)}, u32[]{:S(2)}) collective-permute-start(bf16[8,4096]{1,0:T(8,128)(2,1)S(1)} %copy.183), channel_id=1, source_target_pairs={{0,1},{1,2},{2,3},{3,4},{4,5},{5,6},{6,7},{7,8},{8,9},{9,10},{10,1... | collective-permute-start | bytes 196616 | tf_op jit(solution)/shard_map/while/body/eval_jaxpr/ppermute | solution.py:19
  161.7 9.7 %collective-permute-start.1 = (f32[8,4096]{1,0:T(8,128)S(1)}, f32[8,4096]{1,0:T(8,128)S(1)}, u32[]{:S(2)}, u32[]{:S(2)}) collective-permute-start(f32[8,4096]{1,0:T(8,128)S(1)} %bitcast.168), channel_id=1, source_target_pairs={{0,1},{1,2},{2,3},{3,4},{4,5},{5,6},{6,7},{7,8},{8,9},{9,10},{10,1... | collective-permute-start | bytes 393224 | tf_op jit(solution)/shard_map/while/body/eval_jaxpr/ppermute | solution.py:19
  172.0 15.1 %collective-permute-start = (bf16[8,4096]{1,0:T(8,128)(2,1)S(1)}, bf16[8,4096]{1,0:T(8,128)(2,1)S(1)}, u32[]{:S(2)}, u32[]{:S(2)}) collective-permute-start(bf16[8,4096]{1,0:T(8,128)(2,1)S(1)} %copy.183), channel_id=1, source_target_pairs={{0,1},{1,2},{2,3},{3,4},{4,5},{5,6},{6,7},{7,8},{8,9},{9,10},{10,1... | collective-permute-start | bytes 196616 | tf_op jit(solution)/shard_map/while/body/eval_jaxpr/ppermute | solution.py:19
  177.4 9.7 %collective-permute-start.1 = (f32[8,4096]{1,0:T(8,128)S(1)}, f32[8,4096]{1,0:T(8,128)S(1)}, u32[]{:S(2)}, u32[]{:S(2)}) collective-permute-start(f32[8,4096]{1,0:T(8,128)S(1)} %bitcast.168), channel_id=1, source_target_pairs={{0,1},{1,2},{2,3},{3,4},{4,5},{5,6},{6,7},{7,8},{8,9},{9,10},{10,1... | collective-permute-start | bytes 393224 | tf_op jit(solution)/shard_map/while/body/eval_jaxpr/ppermute | solution.py:19
  187.7 15.1 %collective-permute-start = (bf16[8,4096]{1,0:T(8,128)(2,1)S(1)}, bf16[8,4096]{1,0:T(8,128)(2,1)S(1)}, u32[]{:S(2)}, u32[]{:S(2)}) collective-permute-start(bf16[8,4096]{1,0:T(8,128)(2,1)S(1)} %copy.183), channel_id=1, source_target_pairs={{0,1},{1,2},{2,3},{3,4},{4,5},{5,6},{6,7},{7,8},{8,9},{9,10},{10,1... | collective-permute-start | bytes 196616 | tf_op jit(solution)/shard_map/while/body/eval_jaxpr/ppermute | solution.py:19
  193.1 9.7 %collective-permute-start.1 = (f32[8,4096]{1,0:T(8,128)S(1)}, f32[8,4096]{1,0:T(8,128)S(1)}, u32[]{:S(2)}, u32[]{:S(2)}) collective-permute-start(f32[8,4096]{1,0:T(8,128)S(1)} %bitcast.168), channel_id=1, source_target_pairs={{0,1},{1,2},{2,3},{3,4},{4,5},{5,6},{6,7},{7,8},{8,9},{9,10},{10,1... | collective-permute-start | bytes 393224 | tf_op jit(solution)/shard_map/while/body/eval_jaxpr/ppermute | solution.py:19
  203.3 15.1 %collective-permute-start = (bf16[8,4096]{1,0:T(8,128)(2,1)S(1)}, bf16[8,4096]{1,0:T(8,128)(2,1)S(1)}, u32[]{:S(2)}, u32[]{:S(2)}) collective-permute-start(bf16[8,4096]{1,0:T(8,128)(2,1)S(1)} %copy.183), channel_id=1, source_target_pairs={{0,1},{1,2},{2,3},{3,4},{4,5},{5,6},{6,7},{7,8},{8,9},{9,10},{10,1... | collective-permute-start | bytes 196616 | tf_op jit(solution)/shard_map/while/body/eval_jaxpr/ppermute | solution.py:19
  208.8 9.7 %collective-permute-start.1 = (f32[8,4096]{1,0:T(8,128)S(1)}, f32[8,4096]{1,0:T(8,128)S(1)}, u32[]{:S(2)}, u32[]{:S(2)}) collective-permute-start(f32[8,4096]{1,0:T(8,128)S(1)} %bitcast.168), channel_id=1, source_target_pairs={{0,1},{1,2},{2,3},{3,4},{4,5},{5,6},{6,7},{7,8},{8,9},{9,10},{10,1... | collective-permute-start | bytes 393224 | tf_op jit(solution)/shard_map/while/body/eval_jaxpr/ppermute | solution.py:19
  219.0 15.1 %collective-permute-start = (bf16[8,4096]{1,0:T(8,128)(2,1)S(1)}, bf16[8,4096]{1,0:T(8,128)(2,1)S(1)}, u32[]{:S(2)}, u32[]{:S(2)}) collective-permute-start(bf16[8,4096]{1,0:T(8,128)(2,1)S(1)} %copy.183), channel_id=1, source_target_pairs={{0,1},{1,2},{2,3},{3,4},{4,5},{5,6},{6,7},{7,8},{8,9},{9,10},{10,1... | collective-permute-start | bytes 196616 | tf_op jit(solution)/shard_map/while/body/eval_jaxpr/ppermute | solution.py:19
  224.5 9.7 %collective-permute-start.1 = (f32[8,4096]{1,0:T(8,128)S(1)}, f32[8,4096]{1,0:T(8,128)S(1)}, u32[]{:S(2)}, u32[]{:S(2)}) collective-permute-start(f32[8,4096]{1,0:T(8,128)S(1)} %bitcast.168), channel_id=1, source_target_pairs={{0,1},{1,2},{2,3},{3,4},{4,5},{5,6},{6,7},{7,8},{8,9},{9,10},{10,1... | collective-permute-start | bytes 393224 | tf_op jit(solution)/shard_map/while/body/eval_jaxpr/ppermute | solution.py:19
  234.7 15.1 %collective-permute-start = (bf16[8,4096]{1,0:T(8,128)(2,1)S(1)}, bf16[8,4096]{1,0:T(8,128)(2,1)S(1)}, u32[]{:S(2)}, u32[]{:S(2)}) collective-permute-start(bf16[8,4096]{1,0:T(8,128)(2,1)S(1)} %copy.183), channel_id=1, source_target_pairs={{0,1},{1,2},{2,3},{3,4},{4,5},{5,6},{6,7},{7,8},{8,9},{9,10},{10,1... | collective-permute-start | bytes 196616 | tf_op jit(solution)/shard_map/while/body/eval_jaxpr/ppermute | solution.py:19
  240.2 9.7 %collective-permute-start.1 = (f32[8,4096]{1,0:T(8,128)S(1)}, f32[8,4096]{1,0:T(8,128)S(1)}, u32[]{:S(2)}, u32[]{:S(2)}) collective-permute-start(f32[8,4096]{1,0:T(8,128)S(1)} %bitcast.168), channel_id=1, source_target_pairs={{0,1},{1,2},{2,3},{3,4},{4,5},{5,6},{6,7},{7,8},{8,9},{9,10},{10,1... | collective-permute-start | bytes 393224 | tf_op jit(solution)/shard_map/while/body/eval_jaxpr/ppermute | solution.py:19
  250.4 15.1 %collective-permute-start = (bf16[8,4096]{1,0:T(8,128)(2,1)S(1)}, bf16[8,4096]{1,0:T(8,128)(2,1)S(1)}, u32[]{:S(2)}, u32[]{:S(2)}) collective-permute-start(bf16[8,4096]{1,0:T(8,128)(2,1)S(1)} %copy.183), channel_id=1, source_target_pairs={{0,1},{1,2},{2,3},{3,4},{4,5},{5,6},{6,7},{7,8},{8,9},{9,10},{10,1... | collective-permute-start | bytes 196616 | tf_op jit(solution)/shard_map/while/body/eval_jaxpr/ppermute | solution.py:19
  255.8 9.7 %collective-permute-start.1 = (f32[8,4096]{1,0:T(8,128)S(1)}, f32[8,4096]{1,0:T(8,128)S(1)}, u32[]{:S(2)}, u32[]{:S(2)}) collective-permute-start(f32[8,4096]{1,0:T(8,128)S(1)} %bitcast.168), channel_id=1, source_target_pairs={{0,1},{1,2},{2,3},{3,4},{4,5},{5,6},{6,7},{7,8},{8,9},{9,10},{10,1... | collective-permute-start | bytes 393224 | tf_op jit(solution)/shard_map/while/body/eval_jaxpr/ppermute | solution.py:19
  266.1 15.1 %collective-permute-start = (bf16[8,4096]{1,0:T(8,128)(2,1)S(1)}, bf16[8,4096]{1,0:T(8,128)(2,1)S(1)}, u32[]{:S(2)}, u32[]{:S(2)}) collective-permute-start(bf16[8,4096]{1,0:T(8,128)(2,1)S(1)} %copy.183), channel_id=1, source_target_pairs={{0,1},{1,2},{2,3},{3,4},{4,5},{5,6},{6,7},{7,8},{8,9},{9,10},{10,1... | collective-permute-start | bytes 196616 | tf_op jit(solution)/shard_map/while/body/eval_jaxpr/ppermute | solution.py:19
  271.5 9.7 %collective-permute-start.1 = (f32[8,4096]{1,0:T(8,128)S(1)}, f32[8,4096]{1,0:T(8,128)S(1)}, u32[]{:S(2)}, u32[]{:S(2)}) collective-permute-start(f32[8,4096]{1,0:T(8,128)S(1)} %bitcast.168), channel_id=1, source_target_pairs={{0,1},{1,2},{2,3},{3,4},{4,5},{5,6},{6,7},{7,8},{8,9},{9,10},{10,1... | collective-permute-start | bytes 393224 | tf_op jit(solution)/shard_map/while/body/eval_jaxpr/ppermute | solution.py:19
  281.8 15.1 %collective-permute-start = (bf16[8,4096]{1,0:T(8,128)(2,1)S(1)}, bf16[8,4096]{1,0:T(8,128)(2,1)S(1)}, u32[]{:S(2)}, u32[]{:S(2)}) collective-permute-start(bf16[8,4096]{1,0:T(8,128)(2,1)S(1)} %copy.183), channel_id=1, source_target_pairs={{0,1},{1,2},{2,3},{3,4},{4,5},{5,6},{6,7},{7,8},{8,9},{9,10},{10,1... | collective-permute-start | bytes 196616 | tf_op jit(solution)/shard_map/while/body/eval_jaxpr/ppermute | solution.py:19
  287.2 9.7 %collective-permute-start.1 = (f32[8,4096]{1,0:T(8,128)S(1)}, f32[8,4096]{1,0:T(8,128)S(1)}, u32[]{:S(2)}, u32[]{:S(2)}) collective-permute-start(f32[8,4096]{1,0:T(8,128)S(1)} %bitcast.168), channel_id=1, source_target_pairs={{0,1},{1,2},{2,3},{3,4},{4,5},{5,6},{6,7},{7,8},{8,9},{9,10},{10,1... | collective-permute-start | bytes 393224 | tf_op jit(solution)/shard_map/while/body/eval_jaxpr/ppermute | solution.py:19
  297.5 15.1 %collective-permute-start = (bf16[8,4096]{1,0:T(8,128)(2,1)S(1)}, bf16[8,4096]{1,0:T(8,128)(2,1)S(1)}, u32[]{:S(2)}, u32[]{:S(2)}) collective-permute-start(bf16[8,4096]{1,0:T(8,128)(2,1)S(1)} %copy.183), channel_id=1, source_target_pairs={{0,1},{1,2},{2,3},{3,4},{4,5},{5,6},{6,7},{7,8},{8,9},{9,10},{10,1... | collective-permute-start | bytes 196616 | tf_op jit(solution)/shard_map/while/body/eval_jaxpr/ppermute | solution.py:19
  302.9 9.7 %collective-permute-start.1 = (f32[8,4096]{1,0:T(8,128)S(1)}, f32[8,4096]{1,0:T(8,128)S(1)}, u32[]{:S(2)}, u32[]{:S(2)}) collective-permute-start(f32[8,4096]{1,0:T(8,128)S(1)} %bitcast.168), channel_id=1, source_target_pairs={{0,1},{1,2},{2,3},{3,4},{4,5},{5,6},{6,7},{7,8},{8,9},{9,10},{10,1... | collective-permute-start | bytes 393224 | tf_op jit(solution)/shard_map/while/body/eval_jaxpr/ppermute | solution.py:19
  313.1 15.1 %collective-permute-start = (bf16[8,4096]{1,0:T(8,128)(2,1)S(1)}, bf16[8,4096]{1,0:T(8,128)(2,1)S(1)}, u32[]{:S(2)}, u32[]{:S(2)}) collective-permute-start(bf16[8,4096]{1,0:T(8,128)(2,1)S(1)} %copy.183), channel_id=1, source_target_pairs={{0,1},{1,2},{2,3},{3,4},{4,5},{5,6},{6,7},{7,8},{8,9},{9,10},{10,1... | collective-permute-start | bytes 196616 | tf_op jit(solution)/shard_map/while/body/eval_jaxpr/ppermute | solution.py:19
  318.6 9.7 %collective-permute-start.1 = (f32[8,4096]{1,0:T(8,128)S(1)}, f32[8,4096]{1,0:T(8,128)S(1)}, u32[]{:S(2)}, u32[]{:S(2)}) collective-permute-start(f32[8,4096]{1,0:T(8,128)S(1)} %bitcast.168), channel_id=1, source_target_pairs={{0,1},{1,2},{2,3},{3,4},{4,5},{5,6},{6,7},{7,8},{8,9},{9,10},{10,1... | collective-permute-start | bytes 393224 | tf_op jit(solution)/shard_map/while/body/eval_jaxpr/ppermute | solution.py:19
  (74 other events, 274.2 us)
Sparse Core Ops, SparseCore 0:
  23.9 58.5 reduce-scatter.1
where the time goes:
time: 353 us; the launch traced here: 349 us
  waiting for transfers between devices  134 us (38%)
  local copies, waits for them, and re-layouts  117 us (33%)
  other arithmetic  50.3 us (14%)
  matrix products  20.7 us (6%)
  between operations  14.3 us (4%)
  starting transfers between devices  11.1 us (3%)
    ppermute x62, waiting for transfers between devices, passed_along(): lax.ppermute(shard, axis, [(i, (i + by) % peers) for i in range(peers)])  86.3 us
    reduce_sum x32, local copies, waits for them, and re-layouts, absorb(): jnp.sum(weights, axis=3)  29.9 us
    reduce_scatter x1, waiting for transfers between devices, on_device(): lax.psum_scatter(jnp.dot(local_rows, kv_weight, preferred_element_type=jn...  28.9 us
    gather x16, local copies, waits for them, and re-layouts, absorb(): allowed = jnp.take(mask_cols, query_pos // BLK, axis=0)  22.3 us
    all_to_all x1, waiting for transfers between devices, on_device(): lax.all_to_all(outgoing, 'owner', split_axis=0, concat_axis=0, tiled=True)  18.6 us
    while x90, local copies, waits for them, and re-layouts  18.3 us
    reshape x16, local copies, waits for them, and re-layouts, absorb(): running = running.reshape(KVH, per_group, row_count)  12.2 us
    add x16, other arithmetic, absorb(): totals_now.reshape(KVH, per_group, row_count) * factor  11.2 us
  transfers between devices with their start and end apart: 64, of which 18 were waited for; matrix products, arithmetic and copies ran while one was open for 42% of the time, Pallas kernels for 0%

commit v1 on v0

v1 whole, which is shorter than its diff:
```python
import functools

import jax
import jax.numpy as jnp
from jax import lax
from jax.experimental import pallas as pl
from jax.experimental.pallas import tpu as pltpu
from jax.sharding import PartitionSpec as P

QH = 32
KVH = 4
HD = 128
BLK = 128
NBD = 8
RCP = 8
SLOTS = 8
CAP = 4
CTX_DEV = 1024
GROUP = QH // KVH
ROWS = GROUP * RCP
TILE = 4
STAT = 16
HIDDEN = -1e30
LOG2E = 1.4426950408889634
FACTOR = HD ** (-0.5) * LOG2E
MESH = pl.DeviceIdType.MESH


def kernel(
    owner_count,
    cycle_size,
    retrieval,
    counts,
    positions,
    position_col,
    mask_cols,
    hidden,
    weight,
    queries,
    spans,
    context,
    attended,
    x_send,
    slots,
    stage,
    every_query,
    red_send,
    red_recv,
    fresh,
    bias,
    values_ones,
    part_send,
    part_recv,
    levels,
    shares,
    x_sent,
    x_came,
    q_sent,
    q_came,
    r_sent,
    r_came,
    p_sent,
    p_came,
):
    me_o = lax.axis_index("owner")
    me = lax.axis_index("ctx")
    group_size = cycle_size * SLOTS
    f32, bf16 = jnp.float32, jnp.bfloat16

    barrier = pltpu.get_barrier_semaphore()

    @pl.loop(1, cycle_size)
    def _(step):
        peer = lax.rem(me + step, cycle_size)
        pl.semaphore_signal(barrier, inc=1, device_id={"ctx": peer}, device_id_type=MESH)

    @pl.loop(1, owner_count)
    def _(step):
        peer = lax.rem(me_o + step, owner_count)
        pl.semaphore_signal(barrier, inc=1, device_id={"owner": peer}, device_id_type=MESH)

    def chosen_slots(request):
        count = counts[request]
        rank = jnp.int32(0)
        chosen = [jnp.int32(0)] * CAP
        for b in range(NBD):
            span = retrieval[request, b]
            mine = (me * NBD + b < count) & (lax.div(span, group_size) == me_o)
            for k in range(CAP):
                chosen[k] = jnp.where(mine & (rank == k), lax.rem(span, SLOTS), chosen[k])
            rank = rank + jnp.where(mine, 1, 0)
        return chosen

    def pack(request, store):
        chosen = chosen_slots(request)
        for h in range(KVH):
            for k in range(CAP):
                for part in range(2):
                    column = (part * KVH + h) * HD
                    store(h, k, part, spans[chosen[k], :, column : column + HD])

    def x_copy(h, step):
        peer = lax.rem(me_o + step, owner_count)
        return pltpu.make_async_remote_copy(
            src_ref=x_send.at[h, peer],
            dst_ref=slots.at[h, pl.ds(me_o * CAP, CAP)],
            send_sem=x_sent.at[h, peer],
            recv_sem=x_came.at[h, me_o],
            device_id={"owner": peer},
            device_id_type=MESH,
        )

    @pl.loop(1, owner_count)
    def _(step):
        peer = lax.rem(me_o + step, owner_count)

        def store(h, k, part, block):
            x_send[h, peer, k, :, part * HD : (part + 1) * HD] = block

        pack(peer, store)

    pl.semaphore_wait(barrier, cycle_size + owner_count - 2)

    for h in range(KVH):

        @pl.loop(1, owner_count)
        def _(step):
            x_copy(h, step).start()

    def q_copy(h, peer):
        return pltpu.make_async_remote_copy(
            src_ref=queries.at[h],
            dst_ref=every_query.at[h, me],
            send_sem=q_sent.at[h, peer],
            recv_sem=q_came.at[h, me],
            device_id={"ctx": peer},
            device_id_type=MESH,
        )

    @pl.loop(0, me)
    def _(peer):
        q_copy(0, peer).start()

    partial = jnp.dot(hidden[...], weight[...], preferred_element_type=f32)
    half = KVH * HD
    for j in range(cycle_size):
        rows = partial[j * RCP : (j + 1) * RCP]
        red_send[j] = jnp.concatenate([rows[:, :half], rows[:, half:]], axis=0).astype(bf16)

    def r_copy(peer):
        return pltpu.make_async_remote_copy(
            src_ref=red_send.at[peer],
            dst_ref=red_recv.at[me],
            send_sem=r_sent.at[peer],
            recv_sem=r_came.at[me],
            device_id={"ctx": peer},
            device_id_type=MESH,
        )

    @pl.loop(1, cycle_size)
    def _(step):
        r_copy(lax.rem(me + step, cycle_size)).start()

    red_recv[me] = red_send[me]

    @pl.loop(1, KVH)
    def _(h):
        @pl.loop(0, me)
        def _(peer):
            q_copy(h, peer).start()

    for h in range(KVH):
        every_query[h, me] = queries[h]

    def store_own(h, k, part, block):
        slots[h, me_o * CAP + k, :, part * HD : (part + 1) * HD] = block

    pack(me_o, store_own)

    my_count = counts[me_o]
    query_total = cycle_size * RCP
    block_total = mask_cols.shape[0]
    index_of = lax.broadcasted_iota(jnp.int32, (query_total, 1), 0) // RCP
    own_place = position_col[...]
    query_pos = index_of * CTX_DEV + own_place
    query_block = index_of * NBD + own_place // BLK
    onehot = (
        lax.broadcasted_iota(jnp.int32, (query_total, block_total), 1) == query_block
    ).astype(f32).astype(bf16)
    lane = lax.broadcasted_iota(jnp.int32, (query_total, BLK), 1)
    mask_float = mask_cols[...].astype(f32)
    for b in range(NBD):
        column = jnp.broadcast_to(mask_float[:, b : b + 1], (block_total, BLK)).astype(bf16)
        allowed = jnp.dot(onehot, column, preferred_element_type=f32)
        key_block = me * NBD + b
        last = jnp.where(key_block < my_count, query_pos, -1)
        seen = (allowed > 0.5) & (key_block * BLK + lane <= last)
        bias[:, b * BLK : (b + 1) * BLK] = jnp.where(seen, 0.0, HIDDEN)

    values_ones[:, HD:] = jnp.ones((CTX_DEV, HD), bf16)

    @pl.loop(1, cycle_size)
    def _(step):
        source = lax.rem(me + step, cycle_size)
        pltpu.make_async_remote_copy(
            src_ref=red_send.at[source],
            dst_ref=red_recv.at[source],
            send_sem=r_sent.at[source],
            recv_sem=r_came.at[source],
            device_id={"ctx": source},
            device_id_type=MESH,
        ).wait_recv()

    total = red_recv[0].astype(f32)
    for c in range(1, cycle_size):
        total = total + red_recv[c].astype(f32)
    fresh[...] = jnp.zeros((KVH, BLK, 2 * HD), bf16)
    for h in range(KVH):
        columns = slice(h * HD, (h + 1) * HD)
        rows = jnp.concatenate([total[:RCP, columns], total[RCP:, columns]], axis=1)
        fresh[h, : 2 * RCP] = jnp.concatenate([rows, jnp.zeros_like(rows)], axis=0).astype(bf16)

    place_lane = lax.broadcasted_iota(jnp.int32, (1, BLK), 1)
    place_row = jnp.full((1, BLK), -1, jnp.int32)
    for i in range(RCP):
        place_row = jnp.where(place_lane == i, positions[0, me * RCP + i], place_row)

    where_from = []
    for b in range(NBD):
        source = lax.div(retrieval[me_o, b], group_size)
        ordinal = jnp.int32(0)
        for a in range(b):
            same = (lax.div(retrieval[me_o, a], group_size) == source) & (
                me * NBD + a < my_count
            )
            ordinal = ordinal + jnp.where(same, 1, 0)
        where_from.append(source * CAP + jnp.minimum(ordinal, CAP - 1))

    def combine(h):
        @pl.loop(0, me)
        def _(source):
            pltpu.make_async_remote_copy(
                src_ref=part_send.at[h, source],
                dst_ref=part_recv.at[h, source],
                send_sem=p_sent.at[h, source],
                recv_sem=p_came.at[h, source],
                device_id={"ctx": source},
                device_id_type=MESH,
            ).wait_recv()

        for c in range(cycle_size):
            pieces = part_recv[h, c, ROWS:, :].astype(f32)
            level = jnp.sum(pieces, axis=0, keepdims=True)
            levels[c : c + 1, :] = jnp.where(c <= me, level, 2 * HIDDEN)
        level = levels[...]
        share = jnp.exp2(level - jnp.max(level, axis=0, keepdims=True))
        share = share / jnp.sum(share, axis=0, keepdims=True)
        if cycle_size < BLK:
            share = jnp.concatenate(
                [share, jnp.zeros((BLK - cycle_size, BLK), f32)], axis=0
            )
        shares[...] = share.T
        mine = shares[pl.ds(lax.rem(me, 2) * ROWS, ROWS), :]
        result = jnp.zeros((ROWS, HD), f32)
        for c in range(cycle_size):
            part = jnp.where(c <= me, part_recv[h, c, :ROWS, :].astype(f32), 0.0)
            result = result + part * mine[:, c : c + 1]
        attended[h] = result.astype(bf16)

    @pl.loop(0, KVH)
    def _(h):
        @pl.loop(1, owner_count)
        def _(step):
            source = lax.rem(me_o + step, owner_count)
            pltpu.make_async_remote_copy(
                src_ref=x_send.at[h, source],
                dst_ref=slots.at[h, pl.ds(source * CAP, CAP)],
                send_sem=x_sent.at[h, source],
                recv_sem=x_came.at[h, source],
                device_id={"owner": source},
                device_id_type=MESH,
            ).wait_recv()

        key_columns = pl.ds(pl.multiple_of(h * HD, HD), HD)
        value_columns = pl.ds(pl.multiple_of((KVH + h) * HD, HD), HD)
        fresh_rows = fresh[h]
        stage[...] = slots[h]
        for b in range(NBD):
            rows = slice(b * BLK, (b + 1) * BLK)
            match = (
                lax.broadcasted_iota(jnp.int32, (BLK, BLK), 0) + b * BLK == place_row
            ).astype(f32)
            replaced = jnp.sum(match, axis=1, keepdims=True) > 0.5
            placed = jnp.dot(match.astype(bf16), fresh_rows, preferred_element_type=f32)
            block = stage[where_from[b]].astype(f32)
            block = jnp.where(me * NBD + b < my_count, block, 0.0)
            block = jnp.where(replaced, placed, block).astype(bf16)
            context[rows, key_columns] = block[:, :HD]
            context[rows, value_columns] = block[:, HD:]
            values_ones[rows, :HD] = block[:, HD:]

        @pl.loop(me + 1, cycle_size)
        def _(source):
            pltpu.make_async_remote_copy(
                src_ref=queries.at[h],
                dst_ref=every_query.at[h, source],
                send_sem=q_sent.at[h, source],
                recv_sem=q_came.at[h, source],
                device_id={"ctx": source},
                device_id_type=MESH,
            ).wait_recv()

        @pl.loop(lax.div(me, TILE), cycle_size // TILE)
        def _(tile):
            query_rows = every_query[h, pl.ds(tile * TILE, TILE)].reshape(TILE * ROWS, HD)
            scores = lax.dot_general(
                query_rows,
                context[:, key_columns],
                (((1,), (1,)), ((), ())),
                preferred_element_type=f32,
            )
            shift = bias[pl.ds(pl.multiple_of(tile * TILE * RCP, TILE * RCP), TILE * RCP), :]
            scores = scores.reshape(TILE, GROUP, RCP, CTX_DEV) + shift.reshape(
                TILE, 1, RCP, CTX_DEV
            )
            scores = scores.reshape(TILE * ROWS, CTX_DEV)
            highest = jnp.max(scores, axis=1, keepdims=True)
            weights = jnp.exp2((scores - highest) * FACTOR).astype(bf16)
            summed = jnp.dot(weights, values_ones[...], preferred_element_type=f32)
            weight_sum = summed[:, HD:]
            outcome = (summed[:, :HD] / weight_sum).astype(bf16)
            level = highest * FACTOR + jnp.log(weight_sum) * LOG2E
            level = level.T[:STAT]
            high = level.astype(bf16).astype(f32)
            middle = (level - high).astype(bf16).astype(f32)
            low = level - high - middle
            row = lax.broadcasted_iota(jnp.int32, level.shape, 0)
            stat = jnp.where(
                row == 0, high, jnp.where(row == 1, middle, jnp.where(row == 2, low, 0.0))
            ).astype(bf16)
            for jj in range(TILE):
                j = tile * TILE + jj
                pair = jj // 2
                part = outcome[jj * ROWS : (jj + 1) * ROWS]
                stat_part = stat[:, pair * BLK : (pair + 1) * BLK]

                @pl.when(j > me)
                def _():
                    part_send[h, j, :ROWS, :] = part
                    part_send[h, j, ROWS:, :] = stat_part
                    pltpu.make_async_remote_copy(
                        src_ref=part_send.at[h, j],
                        dst_ref=part_recv.at[h, me],
                        send_sem=p_sent.at[h, j],
                        recv_sem=p_came.at[h, me],
                        device_id={"ctx": j},
                        device_id_type=MESH,
                    ).start()

                @pl.when(j == me)
                def _():
                    part_recv[h, me, :ROWS, :] = part
                    part_recv[h, me, ROWS:, :] = stat_part

        @pl.when(h > 0)
        def _():
            combine(h - 1)

    combine(KVH - 1)

    @pl.loop(0, KVH)
    def _(h):
        @pl.loop(1, owner_count)
        def _(step):
            x_copy(h, step).wait_send()

        @pl.loop(0, me)
        def _(peer):
            q_copy(h, peer).wait_send()

        @pl.loop(me + 1, cycle_size)
        def _(j):
            pltpu.make_async_remote_copy(
                src_ref=part_send.at[h, j],
                dst_ref=part_recv.at[h, me],
                send_sem=p_sent.at[h, j],
                recv_sem=p_came.at[h, me],
                device_id={"ctx": j},
                device_id_type=MESH,
            ).wait_send()

    @pl.loop(1, cycle_size)
    def _(step):
        r_copy(lax.rem(me + step, cycle_size)).wait_send()


def on_device(span_cache, retrieval, counts, recompute_pos, hidden, kv_weight, queries, block_mask):
    owner_count = lax.axis_size("owner")
    cycle_size = lax.axis_size("ctx")
    width = span_cache.shape[2]
    bf16 = jnp.bfloat16
    grouped = queries[0].reshape(RCP, KVH, GROUP, HD).transpose(1, 2, 0, 3)
    grouped = grouped.reshape(KVH, ROWS, HD)
    vmem = pl.BlockSpec(memory_space=pltpu.VMEM)
    smem = pl.BlockSpec(memory_space=pltpu.SMEM)
    dma = pltpu.SemaphoreType.DMA
    context, attended = pl.pallas_call(
        functools.partial(kernel, owner_count, cycle_size),
        out_shape=(
            jax.ShapeDtypeStruct((CTX_DEV, width), bf16),
            jax.ShapeDtypeStruct((KVH, ROWS, HD), bf16),
        ),
        in_specs=[smem] * 3 + [vmem] * 6,
        out_specs=(vmem, vmem),
        scratch_shapes=[
            pltpu.VMEM((KVH, owner_count, CAP, BLK, 2 * HD), bf16),
            pltpu.VMEM((KVH, owner_count * CAP, BLK, 2 * HD), bf16),
            pltpu.VMEM((owner_count * CAP, BLK, 2 * HD), bf16),
            pltpu.VMEM((KVH, cycle_size, ROWS, HD), bf16),
            pltpu.VMEM((cycle_size, 2 * RCP, KVH * HD), bf16),
            pltpu.VMEM((cycle_size, 2 * RCP, KVH * HD), bf16),
            pltpu.VMEM((KVH, BLK, 2 * HD), bf16),
            pltpu.VMEM((cycle_size * RCP, CTX_DEV), jnp.float32),
            pltpu.VMEM((CTX_DEV, 2 * HD), bf16),
            pltpu.VMEM((KVH, cycle_size, ROWS + STAT, HD), bf16),
            pltpu.VMEM((KVH, cycle_size, ROWS + STAT, HD), bf16),
            pltpu.VMEM((cycle_size, BLK), jnp.float32),
            pltpu.VMEM((BLK, BLK), jnp.float32),
            dma((KVH, owner_count)),
            dma((KVH, owner_count)),
            dma((KVH, cycle_size)),
            dma((KVH, cycle_size)),
            dma((cycle_size,)),
            dma((cycle_size,)),
            dma((KVH, cycle_size)),
            dma((KVH, cycle_size)),
        ],
        compiler_params=pltpu.CompilerParams(
            collective_id=0, has_side_effects=True, vmem_limit_bytes=56 * 1024 * 1024
        ),
        name="span_attention",
    )(
        retrieval,
        counts,
        recompute_pos,
        recompute_pos.reshape(-1, 1),
        block_mask[0],
        hidden[0],
        kv_weight,
        grouped,
        span_cache,
    )
    attended = attended.reshape(KVH, GROUP, RCP, HD).transpose(2, 0, 1, 3)
    return (context[None], attended.reshape(1, RCP, QH * HD))


def solution(mesh):
    in_specs = (
        P(("owner", "ctx"), None, None),
        P(None, "ctx"),
        P(),
        P("owner", None),
        P("owner", None, "ctx"),
        P("ctx", None),
        P("owner", "ctx", None),
        P("owner", None, "ctx"),
    )
    out_specs = (P("owner", "ctx", None), P("owner", "ctx", None))
    return jax.shard_map(
        on_device, mesh=mesh, in_specs=in_specs, out_specs=out_specs, check_vma=False
    )
```

time: 353 us -> 68 us (0.19)
  the two profiles are of different devices: /device:TPU:0 before, /device:TPU:27 now
where the time goes in v1:
time: 68 us; the launch traced here: 67.8 us
  Pallas kernels  60.6 us (89%)
  local copies, waits for them, and re-layouts  6.55 us (10%)
    pallas_call x1, Pallas kernels, on_device(): pl.pallas_call(functools.partial(kernel, owner_count, cycle_size), out_sh...  60.6 us
    unnamed x5, local copies, waits for them, and re-layouts  5.16 us
    reshape x1, local copies, waits for them, and re-layouts, on_device(): recompute_pos.reshape(-1, 1)  1.39 us

profile of v1, /device:TPU:27, one launch (start us, length us, event | category | flops | bytes accessed | tf_op | source)
XLA Modules:
  0.0 67.8 jit_solution(10829760622683578891)
XLA Ops:
  0.6 1.4 %copy.10 = s32[1,128,8]{2,1,0:T(8,128)} copy(s32[1,128,8]{1,2,0:T(8,128)} %param.15) | data formatting | bytes 8192 | tf_op args[7]
  2.0 1.4 %copy.11.position_col = s32[128,1]{1,0:T(8,128)} copy(s32[128,1]{0,1:T(1,128)} %bitcast.19) | data formatting | bytes 1024 | tf_op jit(solution)/shard_map/reshape | solution.py:446
  3.4 60.6 %span_attention.1 = (bf16[1024,1024]{1,0:T(8,128)(2,1)}, bf16[4,64,128]{2,1,0:T(8,128)(2,1)}) custom-call(s32[2,8]{1,0:T(2,128)} %retrieval.1, s32[2]{0:T(128)} %counts.1, s32[1,128]{1,0:T(1,128)} %positions.1, s32[128,1]{1,0:T(8,128)} %copy.11.position_col, s32[128,8]{1,0:T(8,128)} %bitcast.15, bf16[128,512]{1,0:T(8,128)(2,1)} %bitcast.16, ...), custom_call_target="tpu_custom_call" | custom-call | tf_op jit(solution)/shard_map/span_attention/pallas_call | solution.py:407
  64.0 0.0 copy-start
  64.0 3.1 %copy.14 = bf16[1,1024,1024]{2,1,0:T(8,128)(2,1)} copy(bf16[1,1024,1024]{2,1,0:T(8,128)(2,1)} %bitcast.14) | data formatting | bytes 4194304
  67.1 0.0 copy-done
  67.1 0.6 copy.15
Async XLA Ops:
  64.0 3.1 %copy-start = (bf16[4,64,128]{2,1,0:T(8,128)(2,1)S(1)}, bf16[4,64,128]{2,1,0:T(8,128)(2,1)}, u32[]{:S(2)}) copy-start(bf16[4,64,128]{2,1,0:T(8,128)(2,1)} %get-tuple-element.5) | copy-start | bytes 196612

commit v2 on v1

v2 whole, which is shorter than its diff:
```python
import functools

import jax
import jax.numpy as jnp
from jax import lax
from jax.experimental import pallas as pl
from jax.experimental.pallas import tpu as pltpu
from jax.sharding import PartitionSpec as P

QH = 32
KVH = 4
HD = 128
BLK = 128
NBD = 8
RCP = 8
SLOTS = 8
CAP = 4
CTX_DEV = 1024
GROUP = QH // KVH
ROWS = GROUP * RCP
TILE = 4
STAT = 16
HIDDEN = -1e30
LOG2E = 1.4426950408889634
FACTOR = HD ** (-0.5) * LOG2E
MESH = pl.DeviceIdType.MESH


def kernel(
    owner_count,
    cycle_size,
    retrieval,
    counts,
    positions,
    position_row,
    mask_rows,
    hidden,
    weight,
    queries,
    spans,
    context_out,
    attended,
    x_send,
    x_recv,
    own,
    stage,
    context,
    every_query,
    red_send,
    red_recv,
    fresh,
    bias,
    sums,
    tops,
    totals,
    part_send,
    part_recv,
    levels,
    shares,
    x_sent,
    x_came,
    q_sent,
    q_came,
    r_sent,
    r_came,
    p_sent,
    p_came,
    out_done,
):
    me_o = lax.axis_index("owner")
    me = lax.axis_index("ctx")
    group_size = cycle_size * SLOTS
    f32, bf16 = jnp.float32, jnp.bfloat16
    own_keys = CAP * BLK + BLK

    barrier = pltpu.get_barrier_semaphore()

    @pl.loop(1, cycle_size)
    def _(step):
        peer = lax.rem(me + step, cycle_size)
        pl.semaphore_signal(barrier, inc=1, device_id={"ctx": peer}, device_id_type=MESH)

    @pl.loop(1, owner_count)
    def _(step):
        peer = lax.rem(me_o + step, owner_count)
        pl.semaphore_signal(barrier, inc=1, device_id={"owner": peer}, device_id_type=MESH)

    def chosen_slots(request):
        count = counts[request]
        rank = jnp.int32(0)
        chosen = [jnp.int32(0)] * CAP
        for b in range(NBD):
            span = retrieval[request, b]
            mine = (me * NBD + b < count) & (lax.div(span, group_size) == me_o)
            for k in range(CAP):
                chosen[k] = jnp.where(mine & (rank == k), lax.rem(span, SLOTS), chosen[k])
            rank = rank + jnp.where(mine, 1, 0)
        return chosen

    def pack(chosen, heads, store):
        for h in heads:
            for k in range(CAP):
                for part in range(2):
                    column = (part * KVH + h) * HD
                    store(h, k, part, spans[chosen[k], :, column : column + HD])

    def x_copy(h, step):
        peer = lax.rem(me_o + step, owner_count)
        return pltpu.make_async_remote_copy(
            src_ref=x_send.at[h, peer],
            dst_ref=x_recv.at[h, me_o],
            send_sem=x_sent.at[h, peer],
            recv_sem=x_came.at[h, me_o],
            device_id={"owner": peer},
            device_id_type=MESH,
        )

    def x_start(h):
        @pl.loop(1, owner_count)
        def _(step):
            x_copy(h, step).start()

    def x_wait_send(h):
        @pl.loop(1, owner_count)
        def _(step):
            x_copy(h, step).wait_send()

    def pack_for_peers(heads):
        @pl.loop(1, owner_count)
        def _(step):
            peer = lax.rem(me_o + step, owner_count)

            def store(h, k, part, block):
                x_send[h, peer, k, :, part * HD : (part + 1) * HD] = block

            pack(chosen_slots(peer), heads, store)

    def q_copy(h, peer):
        return pltpu.make_async_remote_copy(
            src_ref=queries.at[h],
            dst_ref=every_query.at[h, me],
            send_sem=q_sent.at[h, peer],
            recv_sem=q_came.at[h, me],
            device_id={"ctx": peer},
            device_id_type=MESH,
        )

    def q_start(h):
        @pl.loop(0, me)
        def _(peer):
            q_copy(h, peer).start()

    def r_copy(peer):
        return pltpu.make_async_remote_copy(
            src_ref=red_send.at[peer],
            dst_ref=red_recv.at[me],
            send_sem=r_sent.at[peer],
            recv_sem=r_came.at[me],
            device_id={"ctx": peer},
            device_id_type=MESH,
        )

    pack_for_peers(range(1))
    pl.semaphore_wait(barrier, cycle_size + owner_count - 2)
    x_start(0)
    q_start(0)
    pack_for_peers(range(1, 2))
    x_start(1)

    partial = jnp.dot(hidden[...], weight[...], preferred_element_type=f32)
    half = KVH * HD
    for j in range(cycle_size):
        rows = partial[j * RCP : (j + 1) * RCP]
        red_send[j] = jnp.concatenate([rows[:, :half], rows[:, half:]], axis=0).astype(bf16)

    @pl.loop(1, cycle_size)
    def _(step):
        r_copy(lax.rem(me + step, cycle_size)).start()

    q_start(1)
    pack_for_peers(range(2, KVH))
    red_recv[me] = red_send[me]

    for h in range(KVH):
        every_query[h, me] = queries[h]

    def store_own(h, k, part, block):
        own[h, k * BLK : (k + 1) * BLK, part * HD : (part + 1) * HD] = block

    pack(chosen_slots(me_o), range(KVH), store_own)

    my_count = counts[me_o]
    query_total = cycle_size * RCP
    block_total = mask_rows.shape[1]

    where_from = []
    usable = []
    for b in range(NBD):
        source = lax.div(retrieval[me_o, b], group_size)
        ordinal = jnp.int32(0)
        for a in range(b):
            same = (lax.div(retrieval[me_o, a], group_size) == source) & (
                me * NBD + a < my_count
            )
            ordinal = ordinal + jnp.where(same, 1, 0)
        where_from.append(source * CAP + jnp.minimum(ordinal, CAP - 1))
        usable.append(me * NBD + b < my_count)

    place_lane = lax.broadcasted_iota(jnp.int32, (1, BLK), 1)
    place_row = jnp.full((1, BLK), -1, jnp.int32)
    for i in range(RCP):
        place_row = jnp.where(place_lane == i, positions[0, me * RCP + i], place_row)
    place_col = jnp.broadcast_to(place_row, (BLK, BLK)).astype(f32).T.astype(jnp.int32)[:, :1]
    block_lane = lax.broadcasted_iota(jnp.int32, (1, BLK), 1)

    index_of = lax.broadcasted_iota(jnp.int32, (1, query_total), 1) // RCP
    own_place = position_row[...]
    query_pos = index_of * CTX_DEV + own_place
    query_block = index_of * NBD + own_place // BLK
    onehot = (
        lax.broadcasted_iota(jnp.int32, (block_total, query_total), 0) == query_block
    ).astype(f32).astype(bf16)
    allowed = jnp.dot(
        mask_rows[...].astype(f32).astype(bf16), onehot, preferred_element_type=f32
    )
    block_row = lax.broadcasted_iota(jnp.int32, (NBD, query_total), 0) + me * NBD
    reach = jnp.where(
        (allowed > 0.5) & (block_row < my_count),
        (query_pos - block_row * BLK).astype(f32),
        -1.0,
    )

    def reach_columns(pieces):
        filled = jnp.concatenate(
            [jnp.broadcast_to(piece, (8, query_total)) for piece in pieces], axis=0
        )
        rest = query_total - filled.shape[0]
        if rest > 0:
            filled = jnp.concatenate([filled, jnp.zeros((rest, query_total), f32)], axis=0)
        return filled.T

    def slot_bias(owner):
        reached = []
        gone = []
        for k in range(CAP):
            slot = jnp.full((1, query_total), -1.0, f32)
            offset = jnp.int32(-1)
            for b in range(NBD):
                here = usable[b] & (where_from[b] == owner * CAP + k)
                slot = jnp.where(here, reach[b : b + 1], slot)
                offset = jnp.where(here, b * BLK, offset)
            reached.append(slot)
            match = (place_col + jnp.zeros((BLK, BLK), jnp.int32)) == block_lane + offset
            row = lax.broadcasted_iota(jnp.int32, (BLK, BLK), 0)
            hit = jnp.where(match & (row < RCP) & (offset >= 0), 1.0, 0.0)
            gone.append(jnp.max(hit, axis=0, keepdims=True))
        columns = reach_columns(reached)
        lanes = block_lane.astype(f32)
        for k in range(CAP):
            seen = (lanes <= columns[:, k * 8 : k * 8 + 1]) & (gone[k] < 0.5)
            bias[owner, :, k * BLK : (k + 1) * BLK] = jnp.where(seen, 0.0, HIDDEN)

    for o in range(owner_count):
        slot_bias(o)

    reached = []
    for i in range(RCP):
        place = positions[0, me * RCP + i]
        row = jnp.full((1, query_total), -1.0, f32)
        for b in range(NBD):
            here = lax.div(place, BLK) == b
            row = jnp.where(here, reach[b : b + 1] - (place - b * BLK).astype(f32), row)
        reached.append(row)
    columns = reach_columns(reached)
    shift = jnp.full((query_total, BLK), HIDDEN, f32)
    for i in range(RCP):
        seen = (columns[:, i * 8 : i * 8 + 1] >= 0.0) & (block_lane == i)
        shift = jnp.where(seen, 0.0, shift)
    bias[me_o, :, CAP * BLK :] = shift

    @pl.loop(1, cycle_size)
    def _(step):
        source = lax.rem(me + step, cycle_size)
        pltpu.make_async_remote_copy(
            src_ref=red_send.at[source],
            dst_ref=red_recv.at[source],
            send_sem=r_sent.at[source],
            recv_sem=r_came.at[source],
            device_id={"ctx": source},
            device_id_type=MESH,
        ).wait_recv()

    total = red_recv[0].astype(f32)
    for c in range(1, cycle_size):
        total = total + red_recv[c].astype(f32)
    fresh[...] = jnp.zeros((KVH, BLK, 2 * HD), bf16)
    for h in range(KVH):
        columns = slice(h * HD, (h + 1) * HD)
        rows = jnp.concatenate([total[:RCP, columns], total[RCP:, columns]], axis=1)
        fresh[h, : 2 * RCP] = jnp.concatenate([rows, jnp.zeros_like(rows)], axis=0).astype(bf16)
        own[h, CAP * BLK :] = fresh[h]

    q_start(2)

    def score(h, tile, keys, owner, key_count):
        query_rows = every_query[h, pl.ds(tile * TILE, TILE)].reshape(TILE * ROWS, HD)
        scores = lax.dot_general(
            query_rows, keys, (((1,), (1,)), ((), ())), preferred_element_type=f32
        )
        first = pl.multiple_of(tile * TILE * RCP, TILE * RCP)
        shift = bias[owner, pl.ds(first, TILE * RCP), :key_count]
        scores = scores.reshape(TILE, GROUP, RCP, key_count) + shift.reshape(
            TILE, 1, RCP, key_count
        )
        return scores.reshape(TILE * ROWS, key_count)

    def tile_rows(tile):
        return pl.ds(pl.multiple_of(tile * TILE * ROWS, TILE * ROWS), TILE * ROWS)

    def attend_own(h):
        @pl.loop(me + 1, cycle_size)
        def _(source):
            pltpu.make_async_remote_copy(
                src_ref=queries.at[h],
                dst_ref=every_query.at[h, source],
                send_sem=q_sent.at[h, source],
                recv_sem=q_came.at[h, source],
                device_id={"ctx": source},
                device_id_type=MESH,
            ).wait_recv()

        @pl.loop(lax.div(me, TILE), cycle_size // TILE)
        def _(tile):
            scores = score(h, tile, own[h, :, :HD], me_o, own_keys)
            highest = jnp.max(scores, axis=1, keepdims=True)
            weights = jnp.exp2((scores - highest) * FACTOR)
            rows = tile_rows(tile)
            totals[h, rows] = jnp.broadcast_to(
                jnp.sum(weights, axis=1, keepdims=True), (TILE * ROWS, HD)
            )
            tops[h, rows] = jnp.broadcast_to(highest, (TILE * ROWS, HD))
            sums[h, rows] = jnp.dot(
                weights.astype(bf16), own[h, :, HD:], preferred_element_type=f32
            )

    def attend_others(h):
        @pl.loop(1, owner_count)
        def _(step):
            source = lax.rem(me_o + step, owner_count)
            pltpu.make_async_remote_copy(
                src_ref=x_send.at[h, source],
                dst_ref=x_recv.at[h, source],
                send_sem=x_sent.at[h, source],
                recv_sem=x_came.at[h, source],
                device_id={"owner": source},
                device_id_type=MESH,
            ).wait_recv()

        @pl.loop(lax.div(me, TILE), cycle_size // TILE)
        def _(tile):
            rows = tile_rows(tile)
            highest, weight_sum, summed = tops[h, rows], totals[h, rows], sums[h, rows]
            for step in range(1, owner_count):
                source = lax.rem(me_o + step, owner_count)
                block = x_recv.at[h, source]
                keys = block[:, :, :HD].reshape(CAP * BLK, HD)
                scores = score(h, tile, keys, source, CAP * BLK)
                newest = jnp.maximum(highest[:, :1], jnp.max(scores, axis=1, keepdims=True))
                weights = jnp.exp2((scores - newest) * FACTOR)
                factor = jnp.exp2((highest - newest) * FACTOR)
                weight_sum = weight_sum * factor + jnp.sum(weights, axis=1, keepdims=True)
                values = block[:, :, HD:].reshape(CAP * BLK, HD)
                summed = summed * factor + jnp.dot(
                    weights.astype(bf16), values, preferred_element_type=f32
                )
                highest = jnp.broadcast_to(newest, (TILE * ROWS, HD))
            outcome = (summed / weight_sum).astype(bf16)
            level = highest * FACTOR + jnp.log(weight_sum) * LOG2E
            level = level.T[:STAT]
            high = level.astype(bf16).astype(f32)
            middle = (level - high).astype(bf16).astype(f32)
            low = level - high - middle
            row = lax.broadcasted_iota(jnp.int32, level.shape, 0)
            stat = jnp.where(
                row == 0, high, jnp.where(row == 1, middle, jnp.where(row == 2, low, 0.0))
            ).astype(bf16)
            for jj in range(TILE):
                j = tile * TILE + jj
                pair = jj // 2
                part = outcome[jj * ROWS : (jj + 1) * ROWS]
                stat_part = stat[:, pair * BLK : (pair + 1) * BLK]

                @pl.when(j > me)
                def _():
                    part_send[h, j, :ROWS, :] = part
                    part_send[h, j, ROWS:, :] = stat_part
                    p_copy(h, j).start()

                @pl.when(j == me)
                def _():
                    part_recv[h, me, :ROWS, :] = part
                    part_recv[h, me, ROWS:, :] = stat_part

    def p_copy(h, j):
        return pltpu.make_async_remote_copy(
            src_ref=part_send.at[h, j],
            dst_ref=part_recv.at[h, me],
            send_sem=p_sent.at[h, j],
            recv_sem=p_came.at[h, me],
            device_id={"ctx": j},
            device_id_type=MESH,
        )

    def out_copies(h):
        for part in range(2):
            columns = pl.ds(pl.multiple_of((part * KVH + h) * HD, HD), HD)
            yield pltpu.make_async_copy(
                context.at[:, columns], context_out.at[:, columns], out_done.at[h, part]
            )

    def assemble(h):
        @pl.loop(1, owner_count)
        def _(step):
            source = lax.rem(me_o + step, owner_count)
            stage[pl.ds(source * CAP, CAP)] = x_recv[h, source]

        stage[pl.ds(me_o * CAP, CAP)] = own[h, : CAP * BLK].reshape(CAP, BLK, 2 * HD)
        fresh_rows = fresh[h]
        for b in range(NBD):
            rows = slice(b * BLK, (b + 1) * BLK)
            match = (
                lax.broadcasted_iota(jnp.int32, (BLK, BLK), 0) + b * BLK == place_row
            ).astype(f32)
            replaced = jnp.sum(match, axis=1, keepdims=True) > 0.5
            placed = jnp.dot(match.astype(bf16), fresh_rows, preferred_element_type=f32)
            block = stage[where_from[b]].astype(f32)
            block = jnp.where(usable[b], block, 0.0)
            block = jnp.where(replaced, placed, block).astype(bf16)
            context[rows, pl.ds(pl.multiple_of(h * HD, HD), HD)] = block[:, :HD]
            context[rows, pl.ds(pl.multiple_of((KVH + h) * HD, HD), HD)] = block[:, HD:]
        for copy in out_copies(h):
            copy.start()

    def combine(h):
        @pl.loop(0, me)
        def _(source):
            pltpu.make_async_remote_copy(
                src_ref=part_send.at[h, source],
                dst_ref=part_recv.at[h, source],
                send_sem=p_sent.at[h, source],
                recv_sem=p_came.at[h, source],
                device_id={"ctx": source},
                device_id_type=MESH,
            ).wait_recv()

        for c in range(cycle_size):
            pieces = part_recv[h, c, ROWS:, :].astype(f32)
            level = jnp.sum(pieces, axis=0, keepdims=True)
            levels[c : c + 1, :] = jnp.where(c <= me, level, 2 * HIDDEN)
        level = levels[...]
        share = jnp.exp2(level - jnp.max(level, axis=0, keepdims=True))
        share = share / jnp.sum(share, axis=0, keepdims=True)
        if cycle_size < BLK:
            share = jnp.concatenate(
                [share, jnp.zeros((BLK - cycle_size, BLK), f32)], axis=0
            )
        shares[...] = share.T
        mine = shares[pl.ds(lax.rem(me, 2) * ROWS, ROWS), :]
        result = jnp.zeros((ROWS, HD), f32)
        for c in range(cycle_size):
            part = jnp.where(c <= me, part_recv[h, c, :ROWS, :].astype(f32), 0.0)
            result = result + part * mine[:, c : c + 1]
        attended[h] = result.astype(bf16)

    attend_own(0)
    q_start(3)
    attend_own(1)
    x_wait_send(0)
    x_start(2)
    attend_others(0)
    x_wait_send(1)
    x_start(3)

    @pl.loop(1, KVH)
    def _(h):
        @pl.when(h < KVH - 1)
        def _():
            attend_own(h + 1)

        assemble(h - 1)
        attend_others(h)
        combine(h - 1)

    assemble(KVH - 1)
    combine(KVH - 1)

    x_wait_send(2)
    x_wait_send(3)

    @pl.loop(0, KVH)
    def _(h):
        for copy in out_copies(h):
            copy.wait()

        @pl.loop(0, me)
        def _(peer):
            q_copy(h, peer).wait_send()

        @pl.loop(me + 1, cycle_size)
        def _(j):
            p_copy(h, j).wait_send()

    @pl.loop(1, cycle_size)
    def _(step):
        r_copy(lax.rem(me + step, cycle_size)).wait_send()


def on_device(span_cache, retrieval, counts, recompute_pos, hidden, kv_weight, queries, block_mask):
    owner_count = lax.axis_size("owner")
    cycle_size = lax.axis_size("ctx")
    width = span_cache.shape[2]
    bf16, f32 = jnp.bfloat16, jnp.float32
    grouped = queries[0].reshape(RCP, KVH, GROUP, HD).transpose(1, 2, 0, 3)
    grouped = grouped.reshape(KVH, ROWS, HD)
    vmem = pl.BlockSpec(memory_space=pltpu.VMEM)
    smem = pl.BlockSpec(memory_space=pltpu.SMEM)
    dma = pltpu.SemaphoreType.DMA
    context, attended = pl.pallas_call(
        functools.partial(kernel, owner_count, cycle_size),
        out_shape=(
            jax.ShapeDtypeStruct((CTX_DEV, width), bf16),
            jax.ShapeDtypeStruct((KVH, ROWS, HD), bf16),
        ),
        in_specs=[smem] * 3 + [vmem] * 6,
        out_specs=(pl.BlockSpec(memory_space=pl.ANY), vmem),
        scratch_shapes=[
            pltpu.VMEM((KVH, owner_count, CAP, BLK, 2 * HD), bf16),
            pltpu.VMEM((KVH, owner_count, CAP, BLK, 2 * HD), bf16),
            pltpu.VMEM((KVH, CAP * BLK + BLK, 2 * HD), bf16),
            pltpu.VMEM((owner_count * CAP, BLK, 2 * HD), bf16),
            pltpu.VMEM((CTX_DEV, width), bf16),
            pltpu.VMEM((KVH, cycle_size, ROWS, HD), bf16),
            pltpu.VMEM((cycle_size, 2 * RCP, KVH * HD), bf16),
            pltpu.VMEM((cycle_size, 2 * RCP, KVH * HD), bf16),
            pltpu.VMEM((KVH, BLK, 2 * HD), bf16),
            pltpu.VMEM((owner_count, cycle_size * RCP, CAP * BLK + BLK), f32),
            pltpu.VMEM((KVH, cycle_size * ROWS, HD), f32),
            pltpu.VMEM((KVH, cycle_size * ROWS, HD), f32),
            pltpu.VMEM((KVH, cycle_size * ROWS, HD), f32),
            pltpu.VMEM((KVH, cycle_size, ROWS + STAT, HD), bf16),
            pltpu.VMEM((KVH, cycle_size, ROWS + STAT, HD), bf16),
            pltpu.VMEM((cycle_size, BLK), f32),
            pltpu.VMEM((BLK, BLK), f32),
            dma((KVH, owner_count)),
            dma((KVH, owner_count)),
            dma((KVH, cycle_size)),
            dma((KVH, cycle_size)),
            dma((cycle_size,)),
            dma((cycle_size,)),
            dma((KVH, cycle_size)),
            dma((KVH, cycle_size)),
            dma((KVH, 2)),
        ],
        compiler_params=pltpu.CompilerParams(
            collective_id=0, has_side_effects=True, vmem_limit_bytes=56 * 1024 * 1024
        ),
        name="span_attention",
    )(
        retrieval,
        counts,
        recompute_pos,
        recompute_pos,
        block_mask[0].T,
        hidden[0],
        kv_weight,
        grouped,
        span_cache,
    )
    attended = attended.reshape(KVH, GROUP, RCP, HD).transpose(2, 0, 1, 3)
    return (context[None], attended.reshape(1, RCP, QH * HD))


def solution(mesh):
    in_specs = (
        P(("owner", "ctx"), None, None),
        P(None, "ctx"),
        P(),
        P("owner", None),
        P("owner", None, "ctx"),
        P("ctx", None),
        P("owner", "ctx", None),
        P("owner", None, "ctx"),
    )
    out_specs = (P("owner", "ctx", None), P("owner", "ctx", None))
    return jax.shard_map(
        on_device, mesh=mesh, in_specs=in_specs, out_specs=out_specs, check_vma=False
    )
```

time: 68 us -> 71.8 us (1.056)
  Pallas kernels: 60.6 us -> 67.2 us
  local copies, waits for them, and re-layouts: 6.55 us -> 3.75 us
    pallas_call x1, Pallas kernels: 60.6 us -> 67.2 us  [on_device(): pl.pallas_call(functools.partial(kernel, owner_count, cycle_size), out_sh...]
    unnamed x5 -> x4, local copies, waits for them, and re-layouts: 5.16 us -> 3.75 us
    reshape x1 -> x0, local copies, waits for them, and re-layouts: 1.39 us -> none  [on_device(): recompute_pos.reshape(-1, 1)]
where the time goes in v2:
time: 71.8 us; the launch traced here: 71.6 us
  Pallas kernels  67.2 us (94%)
  local copies, waits for them, and re-layouts  3.75 us (5%)
    pallas_call x1, Pallas kernels, on_device(): pl.pallas_call(functools.partial(kernel, owner_count, cycle_size), out_sh...  67.2 us
    unnamed x4, local copies, waits for them, and re-layouts  3.75 us

profile of v2, /device:TPU:27, one launch (start us, length us, event | category | flops | bytes accessed | tf_op | source)
XLA Modules:
  0.0 71.6 jit_solution(17646248390188346867)
XLA Ops:
  0.6 67.2 %span_attention.1 = (bf16[1024,1024]{1,0:T(8,128)(2,1)}, bf16[4,64,128]{2,1,0:T(8,128)(2,1)}) custom-call(s32[2,8]{1,0:T(2,128)} %retrieval.1, s32[2]{0:T(128)} %counts.1, s32[1,128]{1,0:T(1,128)} %position_row.1, s32[1,128]{1,0:T(1,128)} %position_row.1, s32[8,128]{1,0:T(8,128)} %bitcast.19, bf16[128,512]{1,0:T(8,128)(2,1)} %bitcast.16, ...), custom_call_target="tpu_custom_call" | custom-call | tf_op jit(solution)/shard_map/span_attention/pallas_call | solution.py:528
  67.9 0.0 copy-start
  67.9 3.1 %copy.12 = bf16[1,1024,1024]{2,1,0:T(8,128)(2,1)} copy(bf16[1,1024,1024]{2,1,0:T(8,128)(2,1)} %bitcast.15) | data formatting | bytes 4194304
  71.0 0.0 copy-done
  71.0 0.6 copy.13
Async XLA Ops:
  67.9 3.1 %copy-start = (bf16[4,64,128]{2,1,0:T(8,128)(2,1)S(1)}, bf16[4,64,128]{2,1,0:T(8,128)(2,1)}, u32[]{:S(2)}) copy-start(bf16[4,64,128]{2,1,0:T(8,128)(2,1)} %get-tuple-element.5) | copy-start | bytes 196612

commit v3 on v2

--- a/solution.py
+++ b/solution.py
@@ -43,6 +43,8 @@
     x_send,
     x_recv,
     own,
+    own_turned,
+    others_turned,
     stage,
     context,
     every_query,
@@ -164,8 +166,9 @@
     pl.semaphore_wait(barrier, cycle_size + owner_count - 2)
     x_start(0)
     q_start(0)
-    pack_for_peers(range(1, 2))
-    x_start(1)
+    pack_for_peers(range(1, KVH))
+    for h in range(1, KVH):
+        x_start(h)
 
     partial = jnp.dot(hidden[...], weight[...], preferred_element_type=f32)
     half = KVH * HD
@@ -177,8 +180,9 @@
     def _(step):
         r_copy(lax.rem(me + step, cycle_size)).start()
 
-    q_start(1)
-    pack_for_peers(range(2, KVH))
+    for h in range(1, KVH):
+        q_start(h)
+
     red_recv[me] = red_send[me]
 
     for h in range(KVH):
@@ -300,12 +304,10 @@
         fresh[h, : 2 * RCP] = jnp.concatenate([rows, jnp.zeros_like(rows)], axis=0).astype(bf16)
         own[h, CAP * BLK :] = fresh[h]
 
-    q_start(2)
-
     def score(h, tile, keys, owner, key_count):
         query_rows = every_query[h, pl.ds(tile * TILE, TILE)].reshape(TILE * ROWS, HD)
         scores = lax.dot_general(
-            query_rows, keys, (((1,), (1,)), ((), ())), preferred_element_type=f32
+            query_rows, keys, (((1,), (0,)), ((), ())), preferred_element_type=f32
         )
         first = pl.multiple_of(tile * TILE * RCP, TILE * RCP)
         shift = bias[owner, pl.ds(first, TILE * RCP), :key_count]
@@ -329,9 +331,11 @@
                 device_id_type=MESH,
             ).wait_recv()
 
+        own_turned[...] = own[h, :, :HD].astype(f32).T.astype(bf16)
+
         @pl.loop(lax.div(me, TILE), cycle_size // TILE)
         def _(tile):
-            scores = score(h, tile, own[h, :, :HD], me_o, own_keys)
+            scores = score(h, tile, own_turned[...], me_o, own_keys)
             highest = jnp.max(scores, axis=1, keepdims=True)
             weights = jnp.exp2((scores - highest) * FACTOR)
             rows = tile_rows(tile)
@@ -355,6 +359,8 @@
                 device_id={"owner": source},
                 device_id_type=MESH,
             ).wait_recv()
+            keys = x_recv[h, source, :, :, :HD].reshape(CAP * BLK, HD)
+            others_turned[source] = keys.astype(f32).T.astype(bf16)
 
         @pl.loop(lax.div(me, TILE), cycle_size // TILE)
         def _(tile):
@@ -363,8 +369,7 @@
             for step in range(1, owner_count):
                 source = lax.rem(me_o + step, owner_count)
                 block = x_recv.at[h, source]
-                keys = block[:, :, :HD].reshape(CAP * BLK, HD)
-                scores = score(h, tile, keys, source, CAP * BLK)
+                scores = score(h, tile, others_turned[source], source, CAP * BLK)
                 newest = jnp.maximum(highest[:, :1], jnp.max(scores, axis=1, keepdims=True))
                 weights = jnp.exp2((scores - newest) * FACTOR)
                 factor = jnp.exp2((highest - newest) * FACTOR)
@@ -473,13 +478,8 @@
         attended[h] = result.astype(bf16)
 
     attend_own(0)
-    q_start(3)
     attend_own(1)
-    x_wait_send(0)
-    x_start(2)
     attend_others(0)
-    x_wait_send(1)
-    x_start(3)
 
     @pl.loop(1, KVH)
     def _(h):
@@ -494,8 +494,8 @@
     assemble(KVH - 1)
     combine(KVH - 1)
 
-    x_wait_send(2)
-    x_wait_send(3)
+    for h in range(KVH):
+        x_wait_send(h)
 
     @pl.loop(0, KVH)
     def _(h):
@@ -537,6 +537,8 @@
             pltpu.VMEM((KVH, owner_count, CAP, BLK, 2 * HD), bf16),
             pltpu.VMEM((KVH, owner_count, CAP, BLK, 2 * HD), bf16),
             pltpu.VMEM((KVH, CAP * BLK + BLK, 2 * HD), bf16),
+            pltpu.VMEM((HD, CAP * BLK + BLK), bf16),
+            pltpu.VMEM((owner_count, HD, CAP * BLK), bf16),
             pltpu.VMEM((owner_count * CAP, BLK, 2 * HD), bf16),
             pltpu.VMEM((CTX_DEV, width), bf16),
             pltpu.VMEM((KVH, cycle_size, ROWS, HD), bf16),

time: 71.8 us -> 71.9 us (level)
  no operation moved by 1% of the time
where the time goes in v3:
time: 71.9 us; the launch traced here: 71.8 us
  Pallas kernels  67.4 us (94%)
  local copies, waits for them, and re-layouts  3.75 us (5%)
    pallas_call x1, Pallas kernels, on_device(): pl.pallas_call(functools.partial(kernel, owner_count, cycle_size), out_sh...  67.4 us
    unnamed x4, local copies, waits for them, and re-layouts  3.75 us

profile of v3, /device:TPU:27, one launch (start us, length us, event | category | flops | bytes accessed | tf_op | source)
XLA Modules:
  0.0 71.8 jit_solution(12709717554008105720)
XLA Ops:
  0.6 67.4 %span_attention.1 = (bf16[1024,1024]{1,0:T(8,128)(2,1)}, bf16[4,64,128]{2,1,0:T(8,128)(2,1)}) custom-call(s32[2,8]{1,0:T(2,128)} %retrieval.1, s32[2]{0:T(128)} %counts.1, s32[1,128]{1,0:T(1,128)} %position_row.1, s32[1,128]{1,0:T(1,128)} %position_row.1, s32[8,128]{1,0:T(8,128)} %bitcast.19, bf16[128,512]{1,0:T(8,128)(2,1)} %bitcast.16, ...), custom_call_target="tpu_custom_call" | custom-call | tf_op jit(solution)/shard_map/span_attention/pallas_call | solution.py:528
  68.0 0.0 copy-start
  68.0 3.1 %copy.12 = bf16[1,1024,1024]{2,1,0:T(8,128)(2,1)} copy(bf16[1,1024,1024]{2,1,0:T(8,128)(2,1)} %bitcast.15) | data formatting | bytes 4194304
  71.1 0.0 copy-done
  71.1 0.6 copy.13
Async XLA Ops:
  68.0 3.1 %copy-start = (bf16[4,64,128]{2,1,0:T(8,128)(2,1)S(1)}, bf16[4,64,128]{2,1,0:T(8,128)(2,1)}, u32[]{:S(2)}) copy-start(bf16[4,64,128]{2,1,0:T(8,128)(2,1)} %get-tuple-element.5) | copy-start | bytes 196612

commit v4 on v1

--- a/solution.py
+++ b/solution.py
@@ -32,17 +32,18 @@
     retrieval,
     counts,
     positions,
-    position_col,
-    mask_cols,
+    position_row,
+    mask_rows,
     hidden,
     weight,
     queries,
     spans,
-    context,
+    context_out,
     attended,
     x_send,
     slots,
     stage,
+    context,
     every_query,
     red_send,
     red_recv,
@@ -61,6 +62,8 @@
     r_came,
     p_sent,
     p_came,
+    f_sent,
+    out_done,
 ):
     me_o = lax.axis_index("owner")
     me = lax.axis_index("ctx")
@@ -137,9 +140,30 @@
             device_id_type=MESH,
         )
 
-    @pl.loop(0, me)
-    def _(peer):
-        q_copy(0, peer).start()
+    my_core = lax.rem(me, 2)
+    my_chip = lax.div(me, 2)
+    sibling = me + 1 - 2 * my_core
+
+    def q_start(h):
+        @pl.when(my_core == 1)
+        def _():
+            q_copy(h, sibling).start()
+
+        @pl.loop(0, my_chip)
+        def _(step):
+            q_copy(h, 2 * (my_chip - 1 - step) + my_core).start()
+
+    def forward(h, source):
+        return pltpu.make_async_remote_copy(
+            src_ref=every_query.at[h, source],
+            dst_ref=every_query.at[h, source],
+            send_sem=f_sent.at[h, source],
+            recv_sem=q_came.at[h, source],
+            device_id={"ctx": sibling},
+            device_id_type=MESH,
+        )
+
+    q_start(0)
 
     partial = jnp.dot(hidden[...], weight[...], preferred_element_type=f32)
     half = KVH * HD
@@ -163,11 +187,8 @@
 
     red_recv[me] = red_send[me]
 
-    @pl.loop(1, KVH)
-    def _(h):
-        @pl.loop(0, me)
-        def _(peer):
-            q_copy(h, peer).start()
+    for h in range(1, KVH):
+        q_start(h)
 
     for h in range(KVH):
         every_query[h, me] = queries[h]
@@ -179,23 +200,31 @@
 
     my_count = counts[me_o]
     query_total = cycle_size * RCP
-    block_total = mask_cols.shape[0]
-    index_of = lax.broadcasted_iota(jnp.int32, (query_total, 1), 0) // RCP
-    own_place = position_col[...]
+    block_total = mask_rows.shape[1]
+    index_of = lax.broadcasted_iota(jnp.int32, (1, query_total), 1) // RCP
+    own_place = position_row[...]
     query_pos = index_of * CTX_DEV + own_place
     query_block = index_of * NBD + own_place // BLK
     onehot = (
-        lax.broadcasted_iota(jnp.int32, (query_total, block_total), 1) == query_block
+        lax.broadcasted_iota(jnp.int32, (block_total, query_total), 0) == query_block
     ).astype(f32).astype(bf16)
-    lane = lax.broadcasted_iota(jnp.int32, (query_total, BLK), 1)
-    mask_float = mask_cols[...].astype(f32)
+    allowed = jnp.dot(
+        mask_rows[...].astype(f32).astype(bf16), onehot, preferred_element_type=f32
+    )
+    block_row = lax.broadcasted_iota(jnp.int32, (NBD, query_total), 0) + me * NBD
+    reach = jnp.where(
+        (allowed > 0.5) & (block_row < my_count),
+        (query_pos - block_row * BLK).astype(f32),
+        -1.0,
+    )
+    if query_total > NBD:
+        reach = jnp.concatenate(
+            [reach, jnp.zeros((query_total - NBD, query_total), f32)], axis=0
+        )
+    reach = reach.T
+    lane = lax.broadcasted_iota(jnp.int32, (1, BLK), 1).astype(f32)
     for b in range(NBD):
-        column = jnp.broadcast_to(mask_float[:, b : b + 1], (block_total, BLK)).astype(bf16)
-        allowed = jnp.dot(onehot, column, preferred_element_type=f32)
-        key_block = me * NBD + b
-        last = jnp.where(key_block < my_count, query_pos, -1)
-        seen = (allowed > 0.5) & (key_block * BLK + lane <= last)
-        bias[:, b * BLK : (b + 1) * BLK] = jnp.where(seen, 0.0, HIDDEN)
+        bias[:, b * BLK : (b + 1) * BLK] = jnp.where(lane <= reach[:, b : b + 1], 0.0, HIDDEN)
 
     values_ones[:, HD:] = jnp.ones((CTX_DEV, HD), bf16)
 
@@ -267,6 +296,20 @@
             result = result + part * mine[:, c : c + 1]
         attended[h] = result.astype(bf16)
 
+    def out_copies(h):
+        for part in range(2):
+            columns = pl.ds(pl.multiple_of((part * KVH + h) * HD, HD), HD)
+            yield pltpu.make_async_copy(
+                context.at[:, columns], context_out.at[:, columns], out_done.at[h, part]
+            )
+
+    def collect(h):
+        @pl.loop(my_chip + 1, cycle_size // 2)
+        def _(chip):
+            arrived = forward(h, 2 * chip + my_core)
+            arrived.wait_recv()
+            arrived.start()
+
     @pl.loop(0, KVH)
     def _(h):
         @pl.loop(1, owner_count)
@@ -299,16 +342,17 @@
             context[rows, value_columns] = block[:, HD:]
             values_ones[rows, :HD] = block[:, HD:]
 
-        @pl.loop(me + 1, cycle_size)
-        def _(source):
-            pltpu.make_async_remote_copy(
-                src_ref=queries.at[h],
-                dst_ref=every_query.at[h, source],
-                send_sem=q_sent.at[h, source],
-                recv_sem=q_came.at[h, source],
-                device_id={"ctx": source},
-                device_id_type=MESH,
-            ).wait_recv()
+        @pl.when(h == 0)
+        def _():
+            collect(h)
+
+        @pl.loop(my_chip + 1, cycle_size // 2)
+        def _(chip):
+            forward(h, 2 * chip + 1 - my_core).wait_recv()
+
+        @pl.when(my_core == 0)
+        def _():
+            forward(h, sibling).wait_recv()
 
         @pl.loop(lax.div(me, TILE), cycle_size // TILE)
         def _(tile):
@@ -362,6 +406,13 @@
                     part_recv[h, me, :ROWS, :] = part
                     part_recv[h, me, ROWS:, :] = stat_part
 
+        for copy in out_copies(h):
+            copy.start()
+
+        @pl.when(h < KVH - 1)
+        def _():
+            collect(h + 1)
+
         @pl.when(h > 0)
         def _():
             combine(h - 1)
@@ -374,9 +425,20 @@
         def _(step):
             x_copy(h, step).wait_send()
 
-        @pl.loop(0, me)
-        def _(peer):
-            q_copy(h, peer).wait_send()
+        for copy in out_copies(h):
+            copy.wait()
+
+        @pl.when(my_core == 1)
+        def _():
+            q_copy(h, sibling).wait_send()
+
+        @pl.loop(0, my_chip)
+        def _(step):
+            q_copy(h, 2 * (my_chip - 1 - step) + my_core).wait_send()
+
+        @pl.loop(my_chip + 1, cycle_size // 2)
+        def _(chip):
+            forward(h, 2 * chip + my_core).wait_send()
 
         @pl.loop(me + 1, cycle_size)
         def _(j):
@@ -411,11 +473,12 @@
             jax.ShapeDtypeStruct((KVH, ROWS, HD), bf16),
         ),
         in_specs=[smem] * 3 + [vmem] * 6,
-        out_specs=(vmem, vmem),
+        out_specs=(pl.BlockSpec(memory_space=pl.ANY), vmem),
         scratch_shapes=[
             pltpu.VMEM((KVH, owner_count, CAP, BLK, 2 * HD), bf16),
             pltpu.VMEM((KVH, owner_count * CAP, BLK, 2 * HD), bf16),
             pltpu.VMEM((owner_count * CAP, BLK, 2 * HD), bf16),
+            pltpu.VMEM((CTX_DEV, width), bf16),
             pltpu.VMEM((KVH, cycle_size, ROWS, HD), bf16),
             pltpu.VMEM((cycle_size, 2 * RCP, KVH * HD), bf16),
             pltpu.VMEM((cycle_size, 2 * RCP, KVH * HD), bf16),
@@ -434,6 +497,8 @@
             dma((cycle_size,)),
             dma((KVH, cycle_size)),
             dma((KVH, cycle_size)),
+            dma((KVH, cycle_size)),
+            dma((KVH, 2)),
         ],
         compiler_params=pltpu.CompilerParams(
             collective_id=0, has_side_effects=True, vmem_limit_bytes=56 * 1024 * 1024
@@ -443,8 +508,8 @@
         retrieval,
         counts,
         recompute_pos,
-        recompute_pos.reshape(-1, 1),
-        block_mask[0],
+        recompute_pos,
+        block_mask[0].T,
         hidden[0],
         kv_weight,
         grouped,

time: 68 us -> 60.5 us (0.89)
  Pallas kernels: 60.6 us -> 56 us
  local copies, waits for them, and re-layouts: 6.55 us -> 3.75 us
    pallas_call x1, Pallas kernels: 60.6 us -> 56 us  [on_device(): pl.pallas_call(functools.partial(kernel, owner_count, cycle_size), out_sh...]
    unnamed x5 -> x4, local copies, waits for them, and re-layouts: 5.16 us -> 3.75 us
    reshape x1 -> x0, local copies, waits for them, and re-layouts: 1.39 us -> none  [on_device(): recompute_pos.reshape(-1, 1)]
where the time goes in v4:
time: 60.5 us; the launch traced here: 60.3 us
  Pallas kernels  56 us (93%)
  local copies, waits for them, and re-layouts  3.75 us (6%)
  between operations  0.65 us (1%)
    pallas_call x1, Pallas kernels, on_device(): pl.pallas_call(functools.partial(kernel, owner_count, cycle_size), out_sh...  56 us
    unnamed x4, local copies, waits for them, and re-layouts  3.75 us

profile of v4, /device:TPU:27, one launch (start us, length us, event | category | flops | bytes accessed | tf_op | source)
XLA Modules:
  0.0 60.3 jit_solution(11343836116823840839)
XLA Ops:
  0.6 56.0 %span_attention.1 = (bf16[1024,1024]{1,0:T(8,128)(2,1)}, bf16[4,64,128]{2,1,0:T(8,128)(2,1)}) custom-call(s32[2,8]{1,0:T(2,128)} %retrieval.1, s32[2]{0:T(128)} %counts.1, s32[1,128]{1,0:T(1,128)} %position_row.1, s32[1,128]{1,0:T(1,128)} %position_row.1, s32[8,128]{1,0:T(8,128)} %bitcast.19, bf16[128,512]{1,0:T(8,128)(2,1)} %bitcast.16, ...), custom_call_target="tpu_custom_call" | custom-call | tf_op jit(solution)/shard_map/span_attention/pallas_call | solution.py:469
  56.6 0.0 copy-start
  56.6 3.1 %copy.12 = bf16[1,1024,1024]{2,1,0:T(8,128)(2,1)} copy(bf16[1,1024,1024]{2,1,0:T(8,128)(2,1)} %bitcast.15) | data formatting | bytes 4194304
  59.7 0.0 copy-done
  59.7 0.6 %copy.13 = bf16[1,8,4096]{2,1,0:T(8,128)(2,1)} copy(bf16[1,8,4096]{2,1,0:T(8,128)(2,1)S(1)} %bitcast.18) | data formatting | bytes 131072
Async XLA Ops:
  56.6 3.1 %copy-start = (bf16[4,64,128]{2,1,0:T(8,128)(2,1)S(1)}, bf16[4,64,128]{2,1,0:T(8,128)(2,1)}, u32[]{:S(2)}) copy-start(bf16[4,64,128]{2,1,0:T(8,128)(2,1)} %get-tuple-element.5) | copy-start | bytes 196612

commit v5 on v4

--- a/solution.py
+++ b/solution.py
@@ -354,8 +354,9 @@
         def _():
             forward(h, sibling).wait_recv()
 
-        @pl.loop(lax.div(me, TILE), cycle_size // TILE)
-        def _(tile):
+        @pl.loop(0, cycle_size // TILE - lax.div(me, TILE))
+        def _(step):
+            tile = cycle_size // TILE - 1 - step
             query_rows = every_query[h, pl.ds(tile * TILE, TILE)].reshape(TILE * ROWS, HD)
             scores = lax.dot_general(
                 query_rows,
@@ -382,7 +383,7 @@
             stat = jnp.where(
                 row == 0, high, jnp.where(row == 1, middle, jnp.where(row == 2, low, 0.0))
             ).astype(bf16)
-            for jj in range(TILE):
+            for jj in reversed(range(TILE)):
                 j = tile * TILE + jj
                 pair = jj // 2
                 part = outcome[jj * ROWS : (jj + 1) * ROWS]

time: 60.5 us -> 60 us (level)
  the two profiles are of different devices: /device:TPU:27 before, /device:TPU:18 now
where the time goes in v5:
time: 60 us; the launch traced here: 59.8 us
  Pallas kernels  55.4 us (92%)
  local copies, waits for them, and re-layouts  3.75 us (6%)
  between operations  0.65 us (1%)
    pallas_call x1, Pallas kernels, on_device(): pl.pallas_call(functools.partial(kernel, owner_count, cycle_size), out_sh...  55.4 us
    unnamed x4, local copies, waits for them, and re-layouts  3.75 us

profile of v5, /device:TPU:18, one launch (start us, length us, event | category | flops | bytes accessed | tf_op | source)
XLA Modules:
  0.0 59.8 jit_solution(13485344499819253844)
XLA Ops:
  0.6 55.4 %span_attention.1 = (bf16[1024,1024]{1,0:T(8,128)(2,1)}, bf16[4,64,128]{2,1,0:T(8,128)(2,1)}) custom-call(s32[2,8]{1,0:T(2,128)} %retrieval.1, s32[2]{0:T(128)} %counts.1, s32[1,128]{1,0:T(1,128)} %position_row.1, s32[1,128]{1,0:T(1,128)} %position_row.1, s32[8,128]{1,0:T(8,128)} %bitcast.19, bf16[128,512]{1,0:T(8,128)(2,1)} %bitcast.16, ...), custom_call_target="tpu_custom_call" | custom-call | tf_op jit(solution)/shard_map/span_attention/pallas_call | solution.py:470
  56.1 0.0 copy-start
  56.1 3.1 %copy.12 = bf16[1,1024,1024]{2,1,0:T(8,128)(2,1)} copy(bf16[1,1024,1024]{2,1,0:T(8,128)(2,1)} %bitcast.15) | data formatting | bytes 4194304
  59.2 0.0 copy-done
  59.2 0.6 %copy.13 = bf16[1,8,4096]{2,1,0:T(8,128)(2,1)} copy(bf16[1,8,4096]{2,1,0:T(8,128)(2,1)S(1)} %bitcast.18) | data formatting | bytes 131072
Async XLA Ops:
  56.1 3.1 %copy-start = (bf16[4,64,128]{2,1,0:T(8,128)(2,1)S(1)}, bf16[4,64,128]{2,1,0:T(8,128)(2,1)}, u32[]{:S(2)}) copy-start(bf16[4,64,128]{2,1,0:T(8,128)(2,1)} %get-tuple-element.5) | copy-start | bytes 196612
